TPU v7x, 32 devices: a whole 2x2x4 slice. The times are simulated.
32 devices in a mesh: blk: 16 (over z, y, x), pts: 2 (over core).
Axes of the slice: x: 2, y: 2, z: 4, core: 2. Of those that a mesh axis runs over, the one named last changes fastest.
Arguments:
- snapshots: float32 [4096, 5, 256], P('blk', None, 'pts'), may hold values from -150 to 150
- weights: float32 [5, 256], P(None, 'pts'), may hold values from 0.3 to 3
- offsets: int32 [16], replicated, may hold values from 0 to 255, as said below
- freqs: int32 [64], replicated, may hold values from 1 to 127, as said below
Outputs:
- modes: float32 [64, 16, 2, 5, 256], P('blk', None, None, None, 'pts')
- spectrum: float32 [64, 16], P('blk')
Inputs may be any that keep to these rules, and one draw needn't show every extreme that they name: Block b covers snapshots b * 256 + offsets[b] onward, 256 of them; the last block's offset is 0 and some other block's is 255. `freqs`: distinct and increasing; 1 and 127 are among them.
All inputs are finite; a program needn't handle non-finite values.
Results may differ from a plain program's by a relative error of at most 0.008.
Values sent between devices are 32-bit elements; how exact they have to be, the bound alone decides.
A program may use at most 64 MiB of HBM per device.

v0:
```python
import math

import jax
import jax.numpy as jnp
from jax import lax
from jax.sharding import PartitionSpec as P

SWEEPS = 2


HIGH = lax.Precision.HIGHEST
DAMPING = 0.01


def passed_along(block, axis, distance):
    devices = range(lax.axis_size(axis))
    route = [(i - distance, i) for i in devices if i - distance in devices]
    return lax.ppermute(block, axis, route)


def spectral_table(freqs, lags, valid, nfft):
    phase_index = jnp.mod(freqs[:, None] * lags[None, :], nfft)
    angle = 2.0 * math.pi / nfft * phase_index.astype(jnp.float32)
    hann = 0.5 - 0.5 * jnp.cos(2.0 * math.pi / nfft * lags.astype(jnp.float32))
    factor = jnp.where(valid, hann, 0.0) / math.sqrt(nfft)
    table = jnp.stack([factor[None, :] * jnp.cos(angle), -factor[None, :] * jnp.sin(angle)], axis=1)
    return table.reshape(2 * freqs.shape[0], nfft)


def rotate_round(carry, round_index):
    real_a, imag_a, real_v, imag_v = carry
    count = real_a.shape[-1]
    index = jnp.arange(count, dtype=jnp.int32)
    mirror = jnp.mod(2 * round_index - index, count - 1)
    partner = jnp.where(
        index == count - 1, round_index, jnp.where(index == round_index, count - 1, mirror)
    )
    parity = jnp.where(index < partner, 1.0, -1.0).astype(jnp.float32)
    diagonal = jnp.diagonal(real_a, axis1=-2, axis2=-1)
    diag_pair = jnp.take(diagonal, partner, axis=-1)
    columns = jnp.broadcast_to(partner[:, None], real_a.shape[:-1] + (1,))
    pair_real = jnp.take_along_axis(real_a, columns, axis=-1)[..., 0]
    pair_imag = jnp.take_along_axis(imag_a, columns, axis=-1)[..., 0]
    delta = parity * (diag_pair - diagonal)
    size_sq = pair_real * pair_real + pair_imag * pair_imag
    radius = jnp.sqrt(delta * delta + 4.0 * size_sq)
    upper = radius + delta + DAMPING * (diagonal + diag_pair)
    length = jnp.sqrt(upper * upper + 4.0 * size_sq)
    cosine = upper / length
    off_real = 2.0 * parity * pair_real / length
    off_imag = 2.0 * parity * pair_imag / length
    moved_real = jnp.take(off_real, partner, axis=-1)
    moved_imag = jnp.take(off_imag, partner, axis=-1)

    def right_apply(left_real, left_imag):
        swap_real = jnp.take(left_real, partner, axis=-1)
        swap_imag = jnp.take(left_imag, partner, axis=-1)
        coef_c = cosine[..., None, :]
        coef_r = moved_real[..., None, :]
        coef_i = moved_imag[..., None, :]
        return (
            left_real * coef_c + swap_real * coef_r - swap_imag * coef_i,
            left_imag * coef_c + swap_real * coef_i + swap_imag * coef_r,
        )

    half_real, half_imag = right_apply(real_a, imag_a)
    swap_real = jnp.take(half_real, partner, axis=-2)
    swap_imag = jnp.take(half_imag, partner, axis=-2)
    coef_c = cosine[..., :, None]
    coef_r = moved_real[..., :, None]
    coef_i = moved_imag[..., :, None]
    new_real = half_real * coef_c + swap_real * coef_r + swap_imag * coef_i
    new_imag = half_imag * coef_c + swap_imag * coef_r - swap_real * coef_i
    vec_real, vec_imag = right_apply(real_v, imag_v)
    return (new_real, new_imag, vec_real, vec_imag)


def jacobi_solve(gram_real, gram_imag):
    count = gram_real.shape[-1]
    identity = jnp.broadcast_to(jnp.eye(count, dtype=gram_real.dtype), gram_real.shape)
    state = (gram_real, gram_imag, identity, jnp.zeros_like(gram_real))

    def advance(counter, carry):
        return rotate_round(carry, jnp.mod(counter, count - 1).astype(jnp.int32))

    return lax.fori_loop(0, SWEEPS * (count - 1), advance, state)


def mode_factors(real_a, real_v, imag_v, nblocks):
    eigen = jnp.diagonal(real_a, axis1=-2, axis2=-1)
    sum_real = jnp.sum(real_v, axis=-2)
    sum_imag = jnp.sum(imag_v, axis=-2)
    magnitude = jnp.sqrt(sum_real * sum_real + sum_imag * sum_imag)
    scaling = 1.0 / (jnp.maximum(magnitude, 1.0) * jnp.sqrt(nblocks * (eigen + 1e-06)))
    phase_real = (sum_real * scaling)[..., None, :]
    phase_imag = (-sum_imag * scaling)[..., None, :]
    coef_real = real_v * phase_real - imag_v * phase_imag
    coef_imag = real_v * phase_imag + imag_v * phase_real
    return (eigen, coef_real, coef_imag)


def body(snapshots, weights, offsets, freqs):
    nfft, nvars, npts = snapshots.shape
    nfreq = freqs.shape[0]
    nblocks = lax.axis_size("blk")
    total_pts = npts * lax.axis_size("pts")
    width = nvars * npts
    block = lax.axis_index("blk")
    lags = jnp.arange(nfft, dtype=jnp.int32)
    flat = snapshots.reshape(nfft, width)
    own_off = offsets[block]
    own_table = spectral_table(freqs, lags - own_off, lags >= own_off, nfft)
    spectra = jnp.dot(own_table, flat, precision=HIGH)
    following = passed_along(flat, "blk", -1)
    tail_table = spectral_table(freqs, lags + nfft - own_off, lags < own_off, nfft)
    spectra = spectra + jnp.dot(tail_table, following, precision=HIGH)
    spectra = spectra.reshape(nfreq, 2, nvars, npts)
    gram_scale = 1.0 / (nblocks * nvars * total_pts)
    grouped = lax.all_to_all(spectra[:, None], "blk", split_axis=0, concat_axis=1, tiled=True)
    local_freqs = grouped.shape[0]
    part_real = grouped[:, :, 0].reshape(local_freqs, nblocks, width)
    part_imag = grouped[:, :, 1].reshape(local_freqs, nblocks, width)
    flat_weights = weights.reshape(1, 1, width)
    weighted_real = part_real * flat_weights
    weighted_imag = part_imag * flat_weights
    gram_real = (
        jnp.einsum("fbx,fcx->fbc", weighted_real, part_real, precision=HIGH)
        + jnp.einsum("fbx,fcx->fbc", weighted_imag, part_imag, precision=HIGH)
    ) * gram_scale
    gram_imag = (
        jnp.einsum("fbx,fcx->fbc", weighted_real, part_imag, precision=HIGH)
        - jnp.einsum("fbx,fcx->fbc", weighted_imag, part_real, precision=HIGH)
    ) * gram_scale
    gram_real, gram_imag = lax.psum((gram_real, gram_imag), "pts")
    real_a, imag_a, real_v, imag_v = jacobi_solve(gram_real, gram_imag)
    eigen, coef_real, coef_imag = mode_factors(real_a, real_v, imag_v, nblocks)
    total = lax.psum(jnp.sum(eigen), "blk")
    mode_real = jnp.einsum("fbx,fbm->fmx", part_real, coef_real, precision=HIGH) - jnp.einsum(
        "fbx,fbm->fmx", part_imag, coef_imag, precision=HIGH
    )
    mode_imag = jnp.einsum("fbx,fbm->fmx", part_real, coef_imag, precision=HIGH) + jnp.einsum(
        "fbx,fbm->fmx", part_imag, coef_real, precision=HIGH
    )
    modes = jnp.stack([mode_real, mode_imag], axis=2).reshape(local_freqs, nblocks, 2, nvars, npts)
    spectrum = nfreq * nblocks * eigen / total
    return (modes, spectrum)


def solution(mesh):
    return jax.shard_map(
        body,
        mesh=mesh,
        in_specs=(P("blk", None, "pts"), P(None, "pts"), P(), P()),
        out_specs=(P("blk", None, None, None, "pts"), P("blk", None)),
        check_vma=False,
    )
```

profile of v0, /device:TPU:0, one launch (start us, length us, event | category | flops | bytes accessed | tf_op | source)
XLA Modules:
  0.0 419.4 jit_solution(16020580195808286903)
XLA Ops:
  0.6 1.3 copy.179
  2.0 1.3 collective-permute-start
  9.0 12.5 %collective-permute-done = f32[256,640]{0,1:T(8,128)S(1)} collective-permute-done((f32[256,640]{0,1:T(8,128)S(1)}, f32[256,640]{0,1:T(8,128)S(1)}, u32[]{:S(2)}, u32[]{:S(2)}) %collective-permute-start) | collective-permute-done | bytes 655392 | tf_op jit(solution)/shard_map/ppermute | solution.py:18
  23.2 7.9 %all-to-all-start = ((f32[64,1,2,5,128]{4,2,3,1,0:T(2,128)}), f32[64,1,2,5,128]{4,2,3,1,0:T(2,128)S(1)}, u32[]{:S(2)}, u32[]{:S(2)}) async-start(f32[64,1,2,5,128]{4,2,3,1,0:T(2,128)} %copy.181), calls=%async_computation | async-start | bytes 655360 | tf_op jit(solution)/shard_map/all_to_all | solution.py:119
  31.2 10.4 %all-to-all-done = f32[64,1,2,5,128]{4,2,3,1,0:T(2,128)S(1)} async-done(((f32[64,1,2,5,128]{4,2,3,1,0:T(2,128)}), f32[64,1,2,5,128]{4,2,3,1,0:T(2,128)S(1)}, u32[]{:S(2)}, u32[]{:S(2)}) %all-to-all-start) | async-done | bytes 327712 | tf_op jit(solution)/shard_map/all_to_all | solution.py:119
  43.8 3.6 all-reduce
  47.8 327.0 %while.20 = (s32[]{:T(128)}, f32[4,16,16]{0,2,1:T(8,128)S(1)}, f32[4,16,16]{0,2,1:T(8,128)S(1)}, f32[4,16,16]{0,2,1:T(8,128)S(1)}, f32[4,16,16]{0,2,1:T(8,128)S(...) while((s32[]{:T(128)}, f32[4,16,16]{0,2,1:T(8,128)S(1)}, f32[4,16,16]{0,2,1:T(8,128)S(1)}, ...), condition=%wide.region_3.8_spmd.clone, body=%wide.region_2.7_spmd.clone.sunk | while | flops 44250 | bytes 254662 | solution.py:86
  48.0 0.9 gather_fusion.2
  49.0 0.9 gather_fusion.3
  58.9 0.9 gather_fusion.2
  59.9 0.9 gather_fusion.3
  69.8 0.9 gather_fusion.2
  70.8 0.9 gather_fusion.3
  80.7 0.9 gather_fusion.2
  81.7 0.9 gather_fusion.3
  91.6 0.9 gather_fusion.2
  92.6 0.9 gather_fusion.3
  102.5 0.9 gather_fusion.2
  103.5 0.9 gather_fusion.3
  113.4 0.9 gather_fusion.2
  114.4 0.9 gather_fusion.3
  124.3 0.9 gather_fusion.2
  125.3 0.9 gather_fusion.3
  135.2 0.9 gather_fusion.2
  136.2 0.9 gather_fusion.3
  146.1 0.9 gather_fusion.2
  147.1 0.9 gather_fusion.3
  157.0 0.9 gather_fusion.2
  288.9 0.9 gather_fusion.3
  299.8 0.9 gather_fusion.3
  376.1 39.3 %psum.23 = f32[]{:T(128)} all-reduce(f32[]{:T(128)} %reduce_sum.29), channel_id=1, replica_groups=mesh['blk'=16,'pts'=2] {'blk'}, use_global_device_ids=true, to_apply=%region_7.12 | all-reduce | flops 1 | bytes 8 | tf_op jit(solution)/shard_map/psum | solution.py:137
  418.4 1.0 copy.189
  (1589 shorter events, 315.5 us)
Async XLA Ops:
  2.0 19.6 %collective-permute-start = (f32[256,640]{0,1:T(8,128)S(1)}, f32[256,640]{0,1:T(8,128)S(1)}, u32[]{:S(2)}, u32[]{:S(2)}) collective-permute-start(f32[256,640]{0,1:T(8,128)S(1)} %bitcast.212), channel_id=1, source_target_pairs={{2,0},{4,2},{6,4},{8,6},{10,8},{12,10},{14,12},{16,14},{18,16},{20... | collective-permute-start | bytes 1966088 | tf_op jit(solution)/shard_map/ppermute | solution.py:18
  3.3 0.7 copy-start.2
  6.6 0.7 copy-start.1
  23.2 18.3 %all-to-all-start = ((f32[64,1,2,5,128]{4,2,3,1,0:T(2,128)}), f32[64,1,2,5,128]{4,2,3,1,0:T(2,128)S(1)}, u32[]{:S(2)}, u32[]{:S(2)}) async-start(f32[64,1,2,5,128]{4,2,3,1,0:T(2,128)} %copy.181), calls=%async_computation | async-start | bytes 655360 | tf_op jit(solution)/shard_map/all_to_all | solution.py:119
  41.7 0.7 copy-start
where the time goes:
time: 420 us; the launch traced here: 419 us
  local copies, waits for them, and re-layouts  320 us (76%)
  blocking collectives  42.9 us (10%)
  waiting for transfers between devices  22.9 us (5%)
  other arithmetic  15.2 us (4%)
  starting transfers between devices  9.19 us (2%)
  loops' own time  4.64 us (1%)
    while x240, local copies, waits for them, and re-layouts  42.9 us
    psum x1, blocking collectives, body(): total = lax.psum(jnp.sum(eigen), 'blk')  39.3 us
    gather x60, local copies, waits for them, and re-layouts, right_apply(): swap_imag = jnp.take(left_imag, partner, axis=-1)  35.2 us
    gather x60, local copies, waits for them, and re-layouts, right_apply(): swap_real = jnp.take(left_real, partner, axis=-1)  35.2 us
    gather x90, local copies, waits for them, and re-layouts, rotate_round(): pair_real = jnp.take_along_axis(real_a, columns, axis=-1)[..., 0]  32.6 us
    gather x60, local copies, waits for them, and re-layouts, rotate_round(): pair_imag = jnp.take_along_axis(imag_a, columns, axis=-1)[..., 0]  30.1 us
    gather x90, local copies, waits for them, and re-layouts, rotate_round(): diagonal = jnp.diagonal(real_a, axis1=-2, axis2=-1)  23.7 us
    gather x60, local copies, waits for them, and re-layouts, rotate_round(): swap_imag = jnp.take(half_imag, partner, axis=-2)  20.4 us
  transfers between devices with their start and end apart: 2, of which 2 were waited for; matrix products, arithmetic and copies ran while one was open for 1% of the time, Pallas kernels for 0%

commit v1 on v0

v1 whole, which is shorter than its diff:
```python
import functools
import math

import jax
import jax.numpy as jnp
from jax import lax
from jax.experimental import pallas as pl
from jax.experimental.pallas import tpu as pltpu
from jax.sharding import PartitionSpec as P

SWEEPS = 2


HIGH = lax.Precision.HIGHEST
DAMPING = 0.01


def passed_along(block, axis, distance):
    devices = range(lax.axis_size(axis))
    route = [(i - distance, i) for i in devices if i - distance in devices]
    return lax.ppermute(block, axis, route)


def spectral_table(freqs, lags, valid, nfft):
    phase_index = jnp.mod(freqs[:, None] * lags[None, :], nfft)
    angle = 2.0 * math.pi / nfft * phase_index.astype(jnp.float32)
    hann = 0.5 - 0.5 * jnp.cos(2.0 * math.pi / nfft * lags.astype(jnp.float32))
    factor = jnp.where(valid, hann, 0.0) / math.sqrt(nfft)
    table = jnp.stack([factor[None, :] * jnp.cos(angle), -factor[None, :] * jnp.sin(angle)], axis=1)
    return table.reshape(2 * freqs.shape[0], nfft)


def half_turned(row, half):
    return pltpu.roll(row, half, 1)


def lane_gather(block, index):
    rows = max(block.shape[0], 8)
    wide = jnp.broadcast_to(block, (rows, block.shape[1]))
    index = jnp.broadcast_to(index, wide.shape)
    return jnp.take_along_axis(wide, index, axis=1, mode="promise_in_bounds")[: block.shape[0]]


def jacobi_on_lanes(gram, count, groups):
    half = groups * count
    lanes = 2 * half
    lane = lax.broadcasted_iota(jnp.int32, (1, lanes), 1)
    column = lax.rem(lane, count)
    first = lane - column
    in_real = lane < half
    sign = jnp.where(in_real, 1.0, -1.0).astype(jnp.float32)
    row = lax.broadcasted_iota(jnp.int32, (count, lanes), 0)
    on_diagonal = row == column
    eye = jnp.where(on_diagonal & in_real, 1.0, 0.0).astype(jnp.float32)
    real_diag = jnp.sum(gram * eye, axis=0, keepdims=True)
    diag = real_diag + half_turned(real_diag, half)

    def advance(counter, carry):
        vec, prod, diag = carry
        turn = lax.rem(counter, count - 1)
        mirror = 2 * turn - column
        mirror = jnp.where(mirror < 0, mirror + (count - 1), mirror)
        mirror = jnp.where(mirror >= count - 1, mirror - (count - 1), mirror)
        partner = jnp.where(column == count - 1, turn, jnp.where(column == turn, count - 1, mirror))
        parity = jnp.where(column < partner, 1.0, -1.0).astype(jnp.float32)
        same = first + partner
        other = jnp.where(same < half, same + half, same - half)
        prod_same = lane_gather(prod, same)
        prod_other = lane_gather(prod, other)
        vec_same = lane_gather(vec, same)
        vec_other = lane_gather(vec, other)
        diag_pair = lane_gather(diag, same)
        pair_real = jnp.sum(vec * prod_same, axis=0, keepdims=True)
        pair_real = pair_real + half_turned(pair_real, half)
        pair_imag = sign * jnp.sum(vec * prod_other, axis=0, keepdims=True)
        pair_imag = pair_imag + half_turned(pair_imag, half)
        delta = parity * (diag_pair - diag)
        size4 = 4.0 * (pair_real * pair_real + pair_imag * pair_imag)
        radius = jnp.sqrt(delta * delta + size4)
        upper = radius + delta + DAMPING * (diag + diag_pair)
        inverse = lax.rsqrt(upper * upper + size4)
        cosine = upper * inverse
        scale = 2.0 * parity * inverse
        coef_r = -scale * pair_real
        coef_i = -sign * scale * pair_imag
        sine_sq = size4 * inverse * inverse
        diag = cosine * cosine * diag + sine_sq * diag_pair - parity * cosine * size4 * inverse
        vec = vec * cosine + vec_same * coef_r + vec_other * coef_i
        prod = prod * cosine + prod_same * coef_r + prod_other * coef_i
        return vec, prod, diag

    vec, _, eigen = lax.fori_loop(0, SWEEPS * (count - 1), advance, (eye, gram, diag))
    sums = jnp.sum(vec, axis=0, keepdims=True)
    turned = half_turned(sums, half)
    magnitude = jnp.sqrt(sums * sums + turned * turned)
    scaling = 1.0 / (jnp.maximum(magnitude, 1.0) * jnp.sqrt(count * (eigen + 1e-06)))
    phase_real = jnp.where(in_real, sums, turned) * scaling
    phase_imag = -jnp.where(in_real, turned, sums) * scaling
    coef = vec * phase_real - half_turned(vec, half) * (sign * phase_imag)
    return coef, eigen


def jacobi_kernel(count, groups, gram_ref, coef_ref, eigen_ref):
    coef, eigen = jacobi_on_lanes(gram_ref[...], count, groups)
    coef_ref[...] = coef
    eigen_ref[...] = jnp.broadcast_to(eigen, eigen_ref.shape)


def jacobi_call(gram_real, gram_imag):
    groups, count, _ = gram_real.shape
    half = groups * count
    gram = jnp.stack([gram_real, gram_imag]).transpose(2, 0, 1, 3).reshape(count, 2 * half)
    coef, eigen = pl.pallas_call(
        functools.partial(jacobi_kernel, count, groups),
        out_shape=(
            jax.ShapeDtypeStruct((count, 2 * half), jnp.float32),
            jax.ShapeDtypeStruct((8, 2 * half), jnp.float32),
        ),
        in_specs=[pl.BlockSpec(memory_space=pltpu.VMEM)],
        out_specs=(pl.BlockSpec(memory_space=pltpu.VMEM), pl.BlockSpec(memory_space=pltpu.VMEM)),
    )(gram)
    coef = coef.reshape(count, 2, groups, count)
    return eigen[0, :half].reshape(groups, count), coef[:, 0].transpose(1, 0, 2), coef[:, 1].transpose(1, 0, 2)


def body(snapshots, weights, offsets, freqs):
    nfft, nvars, npts = snapshots.shape
    nfreq = freqs.shape[0]
    nblocks = lax.axis_size("blk")
    total_pts = npts * lax.axis_size("pts")
    width = nvars * npts
    block = lax.axis_index("blk")
    lags = jnp.arange(nfft, dtype=jnp.int32)
    flat = snapshots.reshape(nfft, width)
    own_off = offsets[block]
    own_table = spectral_table(freqs, lags - own_off, lags >= own_off, nfft)
    spectra = jnp.dot(own_table, flat, precision=HIGH)
    following = passed_along(flat, "blk", -1)
    tail_table = spectral_table(freqs, lags + nfft - own_off, lags < own_off, nfft)
    spectra = spectra + jnp.dot(tail_table, following, precision=HIGH)
    spectra = spectra.reshape(nfreq, 2, nvars, npts)
    gram_scale = 1.0 / (nblocks * nvars * total_pts)
    grouped = lax.all_to_all(spectra[:, None], "blk", split_axis=0, concat_axis=1, tiled=True)
    local_freqs = grouped.shape[0]
    part_real = grouped[:, :, 0].reshape(local_freqs, nblocks, width)
    part_imag = grouped[:, :, 1].reshape(local_freqs, nblocks, width)
    flat_weights = weights.reshape(1, 1, width)
    weighted_real = part_real * flat_weights
    weighted_imag = part_imag * flat_weights
    gram_real = (
        jnp.einsum("fbx,fcx->fbc", weighted_real, part_real, precision=HIGH)
        + jnp.einsum("fbx,fcx->fbc", weighted_imag, part_imag, precision=HIGH)
    ) * gram_scale
    gram_imag = (
        jnp.einsum("fbx,fcx->fbc", weighted_real, part_imag, precision=HIGH)
        - jnp.einsum("fbx,fcx->fbc", weighted_imag, part_real, precision=HIGH)
    ) * gram_scale
    gram_real, gram_imag = lax.psum((gram_real, gram_imag), "pts")
    total = lax.psum(jnp.sum(jnp.diagonal(gram_real, axis1=-2, axis2=-1)), "blk")
    eigen, coef_real, coef_imag = jacobi_call(gram_real, gram_imag)
    mode_real = jnp.einsum("fbx,fbm->fmx", part_real, coef_real, precision=HIGH) - jnp.einsum(
        "fbx,fbm->fmx", part_imag, coef_imag, precision=HIGH
    )
    mode_imag = jnp.einsum("fbx,fbm->fmx", part_real, coef_imag, precision=HIGH) + jnp.einsum(
        "fbx,fbm->fmx", part_imag, coef_real, precision=HIGH
    )
    modes = jnp.stack([mode_real, mode_imag], axis=2).reshape(local_freqs, nblocks, 2, nvars, npts)
    spectrum = nfreq * nblocks * eigen / total
    return (modes, spectrum)


def solution(mesh):
    return jax.shard_map(
        body,
        mesh=mesh,
        in_specs=(P("blk", None, "pts"), P(None, "pts"), P(), P()),
        out_specs=(P("blk", None, None, None, "pts"), P("blk", None)),
        check_vma=False,
    )
```

time: 420 us -> 102 us (0.24)
  local copies, waits for them, and re-layouts: 320 us -> 9.37 us
  other arithmetic: 15.2 us -> 4.69 us
  Pallas kernels: 0 us -> 7.23 us
  loops' own time: 4.64 us -> 0 us
    gather x601 -> x1, local copies, waits for them, and re-layouts: 251 us -> 0.62 us  [body(): jnp.diagonal(gram_real, axis1=-2, axis2=-1)]
    while x240 -> x0, local copies, waits for them, and re-layouts: 42.9 us -> none
    pallas_call x0 -> x1, Pallas kernels: none -> 7.23 us  [jacobi_call(): pl.pallas_call(functools.partial(jacobi_kernel, count, groups), out_shape...]
    div x90 -> x1, local copies, waits for them, and re-layouts: 7.5 us -> 0.67 us  [body(): spectrum = nfreq * nblocks * eigen / total]
    select_n x60 -> x0, local copies, waits for them, and re-layouts: 4.74 us -> none  [the longest x30 2.37 us: rotate_round(): moved_real = jnp.take(off_real, partner, axis=-1)]
    another operation x1 -> x0, loops' own time: 4.64 us -> none  [jacobi_solve(): return lax.fori_loop(0, SWEEPS * (count - 1), advance, state)]
    add x60 -> x0, other arithmetic: 4.22 us -> none  [the longest x30 4.08 us: right_apply(): left_imag * coef_c + swap_real * coef_i + swap_imag * coef_r]
  transfers between devices with their start and end apart: 2 -> 2, of which waited for: 2 -> 2; matrix products, arithmetic and copies ran while one was open for 1% -> 4% of each run, Pallas kernels for 0% -> 0%
where the time goes in v1:
time: 102 us; the launch traced here: 101 us
  blocking collectives  42.9 us (42%)
  waiting for transfers between devices  22.9 us (22%)
  local copies, waits for them, and re-layouts  9.37 us (9%)
  starting transfers between devices  9.19 us (9%)
  Pallas kernels  7.23 us (7%)
  other arithmetic  4.69 us (5%)
  matrix products  3.93 us (4%)
    psum x1, blocking collectives, body(): lax.psum(jnp.sum(jnp.diagonal(gram_real, axis1=-2, axis2=-1)), 'blk')  39.3 us
    ppermute x1, waiting for transfers between devices, passed_along(): return lax.ppermute(block, axis, route)  12.5 us
    all_to_all x1, waiting for transfers between devices, body(): lax.all_to_all(spectra[:, None], 'blk', split_axis=0, concat_axis=1, tile...  10.4 us
    all_to_all x1, starting transfers between devices, body(): lax.all_to_all(spectra[:, None], 'blk', split_axis=0, concat_axis=1, tile...  7.9 us
    pallas_call x1, Pallas kernels, jacobi_call(): pl.pallas_call(functools.partial(jacobi_kernel, count, groups), out_shape...  7.23 us
    unnamed x8, local copies, waits for them, and re-layouts  4.22 us
    psum x1, blocking collectives, body(): gram_real, gram_imag = lax.psum((gram_real, gram_imag), 'pts')  3.6 us
  transfers between devices with their start and end apart: 2, of which 2 were waited for; matrix products, arithmetic and copies ran while one was open for 4% of the time, Pallas kernels for 0%

profile of v1, /device:TPU:0, one launch (start us, length us, event | category | flops | bytes accessed | tf_op | source)
XLA Modules:
  0.0 101.1 jit_solution(8396658706963459101)
XLA Ops:
  0.6 1.3 %copy.37 = f32[256,5,128]{0,2,1:T(8,128)S(1)} copy(f32[256,5,128]{2,0,1:T(8,128)} %param.4) | data formatting | bytes 1310720 | tf_op args[0]
  2.0 1.3 %collective-permute-start = (f32[256,640]{0,1:T(8,128)S(1)}, f32[256,640]{0,1:T(8,128)S(1)}, u32[]{:S(2)}, u32[]{:S(2)}) collective-permute-start(f32[256,640]{0,1:T(8,128)S(1)} %bitcast.45), channel_id=1, source_target_pairs={{2,0},{4,2},{6,4},{8,6},{10,8},{12,10},{14,12},{16,14},{18,16},{20... | collective-permute-start | bytes 1966088 | tf_op jit(solution)/shard_map/ppermute | solution.py:21
  3.3 0.6 copy-done.2
  3.9 0.6 dynamic_slice.3
  4.5 0.7 fusion.21
  5.2 0.7 add_subtract_fusion
  5.9 0.7 fusion.23
  6.6 0.6 copy-done.1
  7.2 0.6 cosine_multiply_fusion
  8.3 0.7 fusion.26
  9.0 12.5 %collective-permute-done = f32[256,640]{0,1:T(8,128)S(1)} collective-permute-done((f32[256,640]{0,1:T(8,128)S(1)}, f32[256,640]{0,1:T(8,128)S(1)}, u32[]{:S(2)}, u32[]{:S(2)}) %collective-permute-start) | collective-permute-done | bytes 655392 | tf_op jit(solution)/shard_map/ppermute | solution.py:21
  21.5 0.7 convolution_add_fusion
  22.3 0.9 copy.39
  23.2 7.9 %all-to-all-start = ((f32[64,1,2,5,128]{4,2,3,1,0:T(2,128)}), f32[64,1,2,5,128]{4,2,3,1,0:T(2,128)S(1)}, u32[]{:S(2)}, u32[]{:S(2)}) async-start(f32[64,1,2,5,128]{4,2,3,1,0:T(2,128)} %copy.39), calls=%async_computation | async-start | bytes 655360 | tf_op jit(solution)/shard_map/all_to_all | solution.py:143
  31.1 10.4 %all-to-all-done = f32[64,1,2,5,128]{4,2,3,1,0:T(2,128)S(1)} async-done(((f32[64,1,2,5,128]{4,2,3,1,0:T(2,128)}), f32[64,1,2,5,128]{4,2,3,1,0:T(2,128)S(1)}, u32[]{:S(2)}, u32[]{:S(2)}) %all-to-all-start) | async-done | bytes 327712 | tf_op jit(solution)/shard_map/all_to_all | solution.py:143
  41.8 0.6 copy-done
  42.4 0.3 fusion.7
  42.8 0.3 fusion.5
  43.1 0.3 fusion
  43.4 0.3 fusion.2
  43.8 3.6 %all-reduce = (f32[1,4,16,16]{3,2,1,0:T(8,128)S(1)}, f32[4,16,16]{2,1,0:T(8,128)S(1)}) all-reduce(f32[1,4,16,16]{3,2,1,0:T(8,128)S(1)} %fusion.2, f32[4,16,16]{2,1,0:T(8,128)S(1)} %fusion), channel_id=1, replica_groups=mesh['blk'=16,'pts'=2] {'pts'}, use_global_device_ids=true, to_apply=%region_1.2 | all-reduce | flops 2048 | bytes 16384 | tf_op jit(solution)/shard_map/psum | solution.py:158
  47.6 0.7 reshape.390.gram_ref
  48.3 7.2 %shard_map.59 = (f32[16,128]{1,0:T(8,128)}, f32[8,128]{1,0:T(8,128)}) custom-call(f32[16,128]{1,0:T(8,128)} %reshape.390.gram_ref), custom_call_target="tpu_custom_call" | custom-call | tf_op jit(solution)/shard_map/pallas_call | solution.py:113
  55.5 0.8 copy.46
  56.6 0.6 gather_fusion
  57.2 0.6 reduce_sum.9
  57.8 0.3 fusion.20
  58.1 39.3 %psum.23 = f32[]{:T(128)} all-reduce(f32[]{:T(128)} %reduce_sum.9), channel_id=1, replica_groups=mesh['blk'=16,'pts'=2] {'blk'}, use_global_device_ids=true, to_apply=%region_3.4 | all-reduce | flops 1 | bytes 8 | tf_op jit(solution)/shard_map/psum | solution.py:159
  97.4 1.3 %divide_reduce_fusion = f32[64]{0:T(128)S(1)} fusion(f32[8,128]{1,0:T(8,128)} %get-tuple-element.5, f32[]{:T(128)} %psum.23), kind=kLoop, calls=%fused_computation.55 | loop fusion | flops 128 | bytes 516 | tf_op jit(solution)/shard_map/div | solution.py:168
  98.8 0.7 div.19
  99.8 0.3 convolution_add_fusion.1
  100.1 1.0 copy.45
  (23 shorter events, 1.5 us)
Async XLA Ops:
  2.0 19.6 %collective-permute-start = (f32[256,640]{0,1:T(8,128)S(1)}, f32[256,640]{0,1:T(8,128)S(1)}, u32[]{:S(2)}, u32[]{:S(2)}) collective-permute-start(f32[256,640]{0,1:T(8,128)S(1)} %bitcast.45), channel_id=1, source_target_pairs={{2,0},{4,2},{6,4},{8,6},{10,8},{12,10},{14,12},{16,14},{18,16},{20... | collective-permute-start | bytes 1966088 | tf_op jit(solution)/shard_map/ppermute | solution.py:21
  3.3 0.7 copy-start.2
  6.6 0.7 copy-start.1
  23.2 18.3 %all-to-all-start = ((f32[64,1,2,5,128]{4,2,3,1,0:T(2,128)}), f32[64,1,2,5,128]{4,2,3,1,0:T(2,128)S(1)}, u32[]{:S(2)}, u32[]{:S(2)}) async-start(f32[64,1,2,5,128]{4,2,3,1,0:T(2,128)} %copy.39), calls=%async_computation | async-start | bytes 655360 | tf_op jit(solution)/shard_map/all_to_all | solution.py:143
  41.7 0.7 copy-start

commit v2 on v1

v2 whole, which is shorter than its diff:
```python
import functools
import math

import jax
import jax.numpy as jnp
from jax import lax
from jax.experimental import pallas as pl
from jax.experimental.pallas import tpu as pltpu
from jax.sharding import PartitionSpec as P

SWEEPS = 2


HIGH = lax.Precision.HIGHEST
DAMPING = 0.01
MESH = pl.DeviceIdType.MESH


def half_turned(row, half):
    return pltpu.roll(row, half, 1)


def lane_gather(block, index):
    rows = max(block.shape[0], 8)
    wide = jnp.broadcast_to(block, (rows, block.shape[1]))
    index = jnp.broadcast_to(index, wide.shape)
    return jnp.take_along_axis(wide, index, axis=1, mode="promise_in_bounds")[: block.shape[0]]


def jacobi_on_lanes(gram, count, groups):
    half = groups * count
    lanes = 2 * half
    lane = lax.broadcasted_iota(jnp.int32, (1, lanes), 1)
    column = lax.rem(lane, count)
    first = lane - column
    in_real = lane < half
    sign = jnp.where(in_real, 1.0, -1.0).astype(jnp.float32)
    row = lax.broadcasted_iota(jnp.int32, (count, lanes), 0)
    on_diagonal = row == column
    eye = jnp.where(on_diagonal & in_real, 1.0, 0.0).astype(jnp.float32)
    real_diag = jnp.sum(gram * eye, axis=0, keepdims=True)
    diag = real_diag + half_turned(real_diag, half)

    def advance(counter, carry):
        vec, prod, diag = carry
        turn = lax.rem(counter, count - 1)
        mirror = 2 * turn - column
        mirror = jnp.where(mirror < 0, mirror + (count - 1), mirror)
        mirror = jnp.where(mirror >= count - 1, mirror - (count - 1), mirror)
        partner = jnp.where(column == count - 1, turn, jnp.where(column == turn, count - 1, mirror))
        parity = jnp.where(column < partner, 1.0, -1.0).astype(jnp.float32)
        same = first + partner
        other = jnp.where(same < half, same + half, same - half)
        prod_same = lane_gather(prod, same)
        prod_other = lane_gather(prod, other)
        vec_same = lane_gather(vec, same)
        vec_other = lane_gather(vec, other)
        diag_pair = lane_gather(diag, same)
        pair_real = jnp.sum(vec * prod_same, axis=0, keepdims=True)
        pair_real = pair_real + half_turned(pair_real, half)
        pair_imag = sign * jnp.sum(vec * prod_other, axis=0, keepdims=True)
        pair_imag = pair_imag + half_turned(pair_imag, half)
        delta = parity * (diag_pair - diag)
        size4 = 4.0 * (pair_real * pair_real + pair_imag * pair_imag)
        radius = jnp.sqrt(delta * delta + size4)
        upper = radius + delta + DAMPING * (diag + diag_pair)
        inverse = lax.rsqrt(upper * upper + size4)
        cosine = upper * inverse
        scale = 2.0 * parity * inverse
        coef_r = -scale * pair_real
        coef_i = -sign * scale * pair_imag
        sine_sq = size4 * inverse * inverse
        diag = cosine * cosine * diag + sine_sq * diag_pair - parity * cosine * size4 * inverse
        vec = vec * cosine + vec_same * coef_r + vec_other * coef_i
        prod = prod * cosine + prod_same * coef_r + prod_other * coef_i
        return vec, prod, diag

    vec, _, eigen = lax.fori_loop(0, SWEEPS * (count - 1), advance, (eye, gram, diag))
    sums = jnp.sum(vec, axis=0, keepdims=True)
    turned = half_turned(sums, half)
    magnitude = jnp.sqrt(sums * sums + turned * turned)
    scaling = 1.0 / (jnp.maximum(magnitude, 1.0) * jnp.sqrt(count * (eigen + 1e-06)))
    phase_real = jnp.where(in_real, sums, turned) * scaling
    phase_imag = -jnp.where(in_real, turned, sums) * scaling
    coef = vec * phase_real - half_turned(vec, half) * (sign * phase_imag)
    return coef, eigen


def signed_wave(base, index):
    lanes = base.shape[1]
    value = lane_gather(base, jnp.bitwise_and(index, lanes - 1))
    return jnp.where(jnp.bitwise_and(index, lanes) == 0, value, -value)


def write_table(table_ref, offsets_ref, freqs_ref, me, groups):
    rows, nfft = table_ref.shape
    half = nfft // 2
    lane = lax.broadcasted_iota(jnp.int32, (8, half), 1)
    sub = lax.broadcasted_iota(jnp.int32, (8, half), 0)
    base = jnp.cos(2.0 * math.pi / nfft * lane.astype(jnp.float32))
    own = offsets_ref[me]
    before = jnp.where(me > 0, offsets_ref[jnp.maximum(me - 1, 0)], 0)
    quarter = jnp.where(lax.rem(sub, 2) == 1, nfft // 4, 0)
    windows = {}
    for tile in range(rows // 8):
        tile_rows = range(8 * tile, 8 * tile + 8)
        pieces = tuple(r % (4 * groups) // (2 * groups) for r in tile_rows)
        freq = [r // (4 * groups) * groups + r % (2 * groups) // 2 for r in tile_rows]
        freq_rows = jnp.full((8, half), freqs_ref[freq[0]], jnp.int32)
        for s in range(2, 8, 2):
            freq_rows = jnp.where(sub >= s, freqs_ref[freq[s]], freq_rows)
        if pieces not in windows:
            tail = jnp.zeros((8, half), jnp.bool_)
            for s in range(8):
                if pieces[s]:
                    tail = tail | (sub == s)
            start = jnp.where(tail, before, own)
            window = []
            for h in range(2):
                lag = lane + h * half - start
                hann = 0.5 - 0.5 * signed_wave(base, lag)
                valid = (tail & (lag < 0)) | (jnp.logical_not(tail) & (lag >= 0))
                window.append((lag, jnp.where(valid, hann, 0.0) / math.sqrt(nfft)))
            windows[pieces] = window
        for h in range(2):
            lag, factor = windows[pieces][h]
            wave = signed_wave(base, freq_rows * lag + quarter)
            table_ref[8 * tile : 8 * tile + 8, h * half : (h + 1) * half] = factor * wave


def pipeline_kernel(
    nblocks, npart, groups, scale, energy,
    snaps_ref, weights_ref, offsets_ref, freqs_ref, modes_ref, spectrum_ref,
    table, stage, recv, spectra, gram_part, total_part,
    send_sem, recv_sem, gram_send, gram_recv, total_send, total_recv,
):
    me = lax.axis_index("blk")
    side = lax.axis_index("pts")
    nfft, nvars, npts = snaps_ref.shape
    rows = 2 * groups * nblocks
    half = rows // 2
    piece = 2 * groups

    def block_peer(k):
        return lax.rem(me + k, nblocks)

    def side_peer(k):
        return lax.rem(side + k, npart)

    barrier = pltpu.get_barrier_semaphore()
    for k in range(1, nblocks):
        pl.semaphore_signal(barrier, inc=1, device_id={"blk": block_peer(k)}, device_id_type=MESH)
    for k in range(1, npart):
        pl.semaphore_signal(barrier, inc=1, device_id={"pts": side_peer(k)}, device_id_type=MESH)

    write_table(table, offsets_ref, freqs_ref, me, groups)
    for v in range(nvars):
        part = jnp.dot(table[...], snaps_ref[:, v, :], precision=HIGH, preferred_element_type=jnp.float32)
        for g in range(nblocks):
            stage[g, :, v * npts : (v + 1) * npts] = part[2 * piece * g : 2 * piece * (g + 1)]

    pl.semaphore_wait(barrier, nblocks - 1 + npart - 1)

    def spectra_copy(k, slot):
        peer = block_peer(k)
        return pltpu.make_async_remote_copy(
            src_ref=stage.at[peer], dst_ref=recv.at[slot], send_sem=send_sem.at[k],
            recv_sem=recv_sem.at[slot], device_id={"blk": peer}, device_id_type=MESH,
        )

    for k in range(1, nblocks):
        spectra_copy(k, me).start()
    recv[me] = stage[me]
    recv[nblocks] = jnp.zeros(recv.shape[1:], jnp.float32)
    for k in range(1, nblocks):
        spectra_copy(k, block_peer(k)).wait_recv()

    for ri in range(2):
        for f in range(groups):
            at = (ri * groups + f) * nblocks
            own = recv[0:nblocks, 2 * f + ri, :]
            tail = recv[1 : nblocks + 1, piece + 2 * f + ri, :]
            spectra[at : at + nblocks, :] = own + tail

    gram_all = jnp.zeros((rows, rows), jnp.float32)
    for v in range(nvars):
        part = spectra[:, v * npts : (v + 1) * npts]
        gram_all = gram_all + lax.dot_general(
            part * weights_ref[v : v + 1, :], part, (((1,), (1,)), ((), ())),
            precision=HIGH, preferred_element_type=jnp.float32,
        )
    lane = lax.broadcasted_iota(jnp.int32, (1, rows), 1)
    sign = jnp.where(lane < half, 1.0, -1.0).astype(jnp.float32)
    group_of = lax.rem(lane, half) // nblocks
    gram = jnp.zeros((nblocks, rows), jnp.float32)
    for f in range(groups):
        upper = gram_all[f * nblocks : (f + 1) * nblocks]
        lower = gram_all[half + f * nblocks : half + (f + 1) * nblocks]
        gram = jnp.where(group_of == f, upper + sign * pltpu.roll(lower, half, 1), gram)
    gram_part[side] = gram * scale

    def gram_copy(k, slot):
        peer = side_peer(k)
        return pltpu.make_async_remote_copy(
            src_ref=gram_part.at[side], dst_ref=gram_part.at[slot], send_sem=gram_send.at[k],
            recv_sem=gram_recv.at[slot], device_id={"pts": peer}, device_id_type=MESH,
        )

    for k in range(1, npart):
        gram_copy(k, side).start()
    for k in range(1, npart):
        gram_copy(k, side_peer(k)).wait_recv()
    gram = gram_part[0]
    for k in range(1, npart):
        gram = gram + gram_part[k]

    row = lax.broadcasted_iota(jnp.int32, (nblocks, rows), 0)
    trace = jnp.where((row == lax.rem(lane, nblocks)) & (lane < half), gram, 0.0)
    trace = jnp.sum(jnp.sum(trace, axis=0, keepdims=True), axis=1, keepdims=True)
    total_part[me] = jnp.broadcast_to(trace, total_part.shape[1:])

    def total_copy(k, slot):
        peer = block_peer(k)
        return pltpu.make_async_remote_copy(
            src_ref=total_part.at[me], dst_ref=total_part.at[slot], send_sem=total_send.at[k],
            recv_sem=total_recv.at[slot], device_id={"blk": peer}, device_id_type=MESH,
        )

    for k in range(1, nblocks):
        total_copy(k, me).start()

    coef, eigen = jacobi_on_lanes(gram, nblocks, groups)

    turned = -sign * half_turned(coef, half)
    pieces = [jnp.where(group_of == f, block, 0.0) for block in (coef, turned) for f in range(groups)]
    mixing = jnp.concatenate(pieces, axis=0).T
    modes_ref[...] = jnp.dot(mixing, spectra[...], precision=HIGH, preferred_element_type=jnp.float32)

    for k in range(1, nblocks):
        total_copy(k, block_peer(k)).wait_recv()
    total = jnp.sum(total_part[...], axis=0)
    spectrum_ref[...] = energy * eigen / total
    for k in range(1, nblocks):
        spectra_copy(k, me).wait_send()
        total_copy(k, me).wait_send()
    for k in range(1, npart):
        gram_copy(k, side).wait_send()


def body(snapshots, weights, offsets, freqs):
    nfft, nvars, npts = snapshots.shape
    nfreq = freqs.shape[0]
    nblocks = lax.axis_size("blk")
    npart = lax.axis_size("pts")
    groups = nfreq // nblocks
    width = nvars * npts
    rows = 2 * nfreq
    scale = 1.0 / (nblocks * nvars * npts * npart)
    dma = pltpu.SemaphoreType.DMA
    vmem = pl.BlockSpec(memory_space=pltpu.VMEM)
    smem = pl.BlockSpec(memory_space=pltpu.SMEM)
    modes, spectrum = pl.pallas_call(
        functools.partial(pipeline_kernel, nblocks, npart, groups, scale, float(nfreq * nblocks)),
        out_shape=(
            jax.ShapeDtypeStruct((rows, width), jnp.float32),
            jax.ShapeDtypeStruct((8, rows), jnp.float32),
        ),
        in_specs=[vmem, vmem, smem, smem],
        out_specs=(vmem, vmem),
        scratch_shapes=[
            pltpu.VMEM((2 * rows, nfft), jnp.float32),
            pltpu.VMEM((nblocks, 4 * groups, width), jnp.float32),
            pltpu.VMEM((nblocks + 1, 4 * groups, width), jnp.float32),
            pltpu.VMEM((rows, width), jnp.float32),
            pltpu.VMEM((npart, nblocks, rows), jnp.float32),
            pltpu.VMEM((nblocks, 8, rows), jnp.float32),
            dma((nblocks,)), dma((nblocks,)),
            dma((npart,)), dma((npart,)),
            dma((nblocks,)), dma((nblocks,)),
        ],
        compiler_params=pltpu.CompilerParams(
            collective_id=0, has_side_effects=True, vmem_limit_bytes=32 * 1024 * 1024
        ),
    )(snapshots, weights, offsets, freqs)
    modes = modes.reshape(2, groups, nblocks, nvars, npts).transpose(1, 2, 0, 3, 4)
    return modes, spectrum[0, :nfreq].reshape(groups, nblocks)


def solution(mesh):
    return jax.shard_map(
        body,
        mesh=mesh,
        in_specs=(P("blk", None, "pts"), P(None, "pts"), P(), P()),
        out_specs=(P("blk", None, None, None, "pts"), P("blk", None)),
        check_vma=False,
    )
```

time: 102 us -> 34.9 us (0.34)
  blocking collectives: 42.9 us -> 0 us
  Pallas kernels: 7.23 us -> 30.8 us
  waiting for transfers between devices: 22.9 us -> 0 us
  starting transfers between devices: 9.19 us -> 0 us
  local copies, waits for them, and re-layouts: 9.37 us -> 3.24 us
  other arithmetic: 4.69 us -> 0 us
  matrix products: 3.93 us -> 0 us
    psum x2 -> x0, blocking collectives: 42.9 us -> none  [the longest x1 39.3 us: body(): lax.psum(jnp.sum(jnp.diagonal(gram_real, axis1=-2, axis2=-1)), 'blk')]
    pallas_call x1, Pallas kernels: 7.23 us -> 30.8 us  [body(): pl.pallas_call(functools.partial(pipeline_kernel, nblocks, npart, groups,...]
    ppermute x1 -> x0, waiting for transfers between devices: 12.5 us -> none  [passed_along(): return lax.ppermute(block, axis, route)]
    all_to_all x1 -> x0, waiting for transfers between devices: 10.4 us -> none  [body(): lax.all_to_all(spectra[:, None], 'blk', split_axis=0, concat_axis=1, tile...]
    all_to_all x1 -> x0, starting transfers between devices: 7.9 us -> none  [body(): lax.all_to_all(spectra[:, None], 'blk', split_axis=0, concat_axis=1, tile...]
    dot_general x10 -> x0, matrix products: 3.93 us -> none  [the longest x1 0.73 us: body(): spectra = jnp.dot(own_table, flat, precision=HIGH)]
    div x2 -> x0, other arithmetic: 2.04 us -> none  [the longest x1 1.34 us: body(): spectrum = nfreq * nblocks * eigen / total]
    unnamed x8, local copies, waits for them, and re-layouts: 4.22 us -> 2.5 us
  transfers between devices with their start and end apart: 2 -> 0, of which waited for: 2 -> 0; matrix products, arithmetic and copies ran while one was open for 4% -> 0% of each run, Pallas kernels for 0% -> 0%
where the time goes in v2:
time: 34.9 us; the launch traced here: 34.7 us
  Pallas kernels  30.8 us (88%)
  local copies, waits for them, and re-layouts  3.24 us (9%)
  between operations  0.69 us (2%)
    pallas_call x1, Pallas kernels, body(): pl.pallas_call(functools.partial(pipeline_kernel, nblocks, npart, groups,...  30.8 us
    unnamed x8, local copies, waits for them, and re-layouts  2.5 us

profile of v2, /device:TPU:0, one launch (start us, length us, event | category | flops | bytes accessed | tf_op | source)
XLA Modules:
  0.0 34.7 jit_solution(4281341101418966922)
XLA Ops:
  0.6 0.0 copy-start.2
  0.6 0.0 copy-start.1
  0.7 0.0 copy-start
  0.7 1.5 %copy.8.snaps_ref = f32[256,5,128]{2,1,0:T(8,128)S(1)} copy(f32[256,5,128]{2,0,1:T(8,128)} %param.4) | data formatting | bytes 1310720 | tf_op args[0]
  2.2 0.0 copy-done.2
  2.2 0.0 copy-done.1
  2.2 0.0 copy-done
  2.2 30.8 %shard_map.59 = (f32[128,640]{1,0:T(8,128)S(1)}, f32[8,128]{1,0:T(8,128)S(1)}) custom-call(f32[256,5,128]{2,1,0:T(8,128)S(1)} %copy.8.snaps_ref, f32[5,128]{1,0:T(8,128)S(1)} %copy-done, s32[16]{0:T(128)S(1)} %copy-done.1, s32[64]{0:T(128)S(1)} %copy-done.2), custom_call_target="tpu_custom_call" | custom-call | tf_op jit(solution)/shard_map/pallas_call | solution.py:262
  33.0 0.7 %reshape_squeeze.3 = f32[4,16]{1,0:T(4,128)} reshape(f32[64]{0:T(128)S(1)} %slice_reduce_fusion) | data formatting | bytes 512 | tf_op jit(solution)/shard_map/reshape;squeeze | solution.py:286
  33.7 0.1 reshape.7
  33.8 1.0 %copy.9 = f32[4,16,2,5,128]{4,2,3,1,0:T(2,128)} copy(f32[4,16,2,5,128]{4,3,1,0,2:T(8,128)S(1)} %bitcast.1) | data formatting | bytes 655360
  (1 shorter events, 0.0 us)
Async XLA Ops:
  0.6 1.5 %copy-start.2 = (s32[64]{0:T(128)S(1)}, s32[64]{0:T(128)}, u32[]{:S(2)}) copy-start(s32[64]{0:T(128)} %freqs_ref.1) | copy-start | bytes 772
  0.6 1.5 %copy-start.1 = (s32[16]{0:T(128)S(1)}, s32[16]{0:T(128)}, u32[]{:S(2)}) copy-start(s32[16]{0:T(128)} %offsets_ref.1) | copy-start | bytes 196
  0.7 1.5 %copy-start = (f32[5,128]{1,0:T(8,128)S(1)}, f32[5,128]{1,0:T(8,128)}, u32[]{:S(2)}) copy-start(f32[5,128]{1,0:T(8,128)} %weights_ref.1) | copy-start | bytes 7684

commit v3 on v2

--- a/solution.py
+++ b/solution.py
@@ -13,6 +13,7 @@
 
 HIGH = lax.Precision.HIGHEST
 DAMPING = 0.01
+CHUNKS = 2
 MESH = pl.DeviceIdType.MESH
 
 
@@ -23,66 +24,76 @@
 def lane_gather(block, index):
     rows = max(block.shape[0], 8)
     wide = jnp.broadcast_to(block, (rows, block.shape[1]))
-    index = jnp.broadcast_to(index, wide.shape)
+    index = index if index.shape == wide.shape else jnp.broadcast_to(index[:1], wide.shape)
     return jnp.take_along_axis(wide, index, axis=1, mode="promise_in_bounds")[: block.shape[0]]
 
 
 def jacobi_on_lanes(gram, count, groups):
     half = groups * count
     lanes = 2 * half
-    lane = lax.broadcasted_iota(jnp.int32, (1, lanes), 1)
+    lane = lax.broadcasted_iota(jnp.int32, (8, lanes), 1)
     column = lax.rem(lane, count)
     first = lane - column
-    in_real = lane < half
-    sign = jnp.where(in_real, 1.0, -1.0).astype(jnp.float32)
+    in_real = lane[:1] < half
     row = lax.broadcasted_iota(jnp.int32, (count, lanes), 0)
-    on_diagonal = row == column
-    eye = jnp.where(on_diagonal & in_real, 1.0, 0.0).astype(jnp.float32)
-    real_diag = jnp.sum(gram * eye, axis=0, keepdims=True)
-    diag = real_diag + half_turned(real_diag, half)
-
-    def advance(counter, carry):
-        vec, prod, diag = carry
-        turn = lax.rem(counter, count - 1)
+    eye = jnp.where(row == column[:1], 1.0, 0.0).astype(jnp.float32)
+    turned = half_turned(gram, half)
+    prod_r = jnp.where(in_real, gram, turned)
+    prod_i = jnp.where(in_real, turned, gram)
+    diag = jnp.sum(prod_r * eye, axis=0, keepdims=True)
+
+    def partner_of(turn):
         mirror = 2 * turn - column
         mirror = jnp.where(mirror < 0, mirror + (count - 1), mirror)
         mirror = jnp.where(mirror >= count - 1, mirror - (count - 1), mirror)
-        partner = jnp.where(column == count - 1, turn, jnp.where(column == turn, count - 1, mirror))
-        parity = jnp.where(column < partner, 1.0, -1.0).astype(jnp.float32)
+        return jnp.where(column == count - 1, turn, jnp.where(column == turn, count - 1, mirror))
+
+    def advance(counter, carry):
+        vec_r, vec_i, prod_r, prod_i, diag, partner = carry
+        following = partner_of(lax.rem(counter + 1, count - 1))
+        parity = jnp.where(column < partner, 1.0, -1.0).astype(jnp.float32)[:1]
         same = first + partner
-        other = jnp.where(same < half, same + half, same - half)
-        prod_same = lane_gather(prod, same)
-        prod_other = lane_gather(prod, other)
-        vec_same = lane_gather(vec, same)
-        vec_other = lane_gather(vec, other)
+        prod_sr = lane_gather(prod_r, same)
+        prod_si = lane_gather(prod_i, same)
         diag_pair = lane_gather(diag, same)
-        pair_real = jnp.sum(vec * prod_same, axis=0, keepdims=True)
-        pair_real = pair_real + half_turned(pair_real, half)
-        pair_imag = sign * jnp.sum(vec * prod_other, axis=0, keepdims=True)
-        pair_imag = pair_imag + half_turned(pair_imag, half)
+        vec_sr = lane_gather(vec_r, same)
+        vec_si = lane_gather(vec_i, same)
+        pair_real = jnp.sum(vec_r * prod_sr + vec_i * prod_si, axis=0, keepdims=True)
+        pair_imag = jnp.sum(vec_r * prod_si - vec_i * prod_sr, axis=0, keepdims=True)
         delta = parity * (diag_pair - diag)
         size4 = 4.0 * (pair_real * pair_real + pair_imag * pair_imag)
         radius = jnp.sqrt(delta * delta + size4)
-        upper = radius + delta + DAMPING * (diag + diag_pair)
+        upper = radius + (delta + DAMPING * (diag + diag_pair))
         inverse = lax.rsqrt(upper * upper + size4)
         cosine = upper * inverse
         scale = 2.0 * parity * inverse
         coef_r = -scale * pair_real
-        coef_i = -sign * scale * pair_imag
+        coef_i = scale * pair_imag
         sine_sq = size4 * inverse * inverse
         diag = cosine * cosine * diag + sine_sq * diag_pair - parity * cosine * size4 * inverse
-        vec = vec * cosine + vec_same * coef_r + vec_other * coef_i
-        prod = prod * cosine + prod_same * coef_r + prod_other * coef_i
-        return vec, prod, diag
-
-    vec, _, eigen = lax.fori_loop(0, SWEEPS * (count - 1), advance, (eye, gram, diag))
-    sums = jnp.sum(vec, axis=0, keepdims=True)
-    turned = half_turned(sums, half)
-    magnitude = jnp.sqrt(sums * sums + turned * turned)
+
+        def turn_pair(real, imag, swap_real, swap_imag):
+            return (
+                real * cosine + (swap_real * coef_r - swap_imag * coef_i),
+                imag * cosine + (swap_real * coef_i + swap_imag * coef_r),
+            )
+
+        prod_r, prod_i = turn_pair(prod_r, prod_i, prod_sr, prod_si)
+        vec_r, vec_i = turn_pair(vec_r, vec_i, vec_sr, vec_si)
+        return vec_r, vec_i, prod_r, prod_i, diag, following
+
+    state = (eye, jnp.zeros_like(eye), prod_r, prod_i, diag, partner_of(0))
+    state = lax.fori_loop(0, SWEEPS * (count - 1), advance, state, unroll=3)
+    vec_r, vec_i, _, _, eigen, _ = state
+    sum_r = jnp.sum(vec_r, axis=0, keepdims=True)
+    sum_i = jnp.sum(vec_i, axis=0, keepdims=True)
+    magnitude = jnp.sqrt(sum_r * sum_r + sum_i * sum_i)
     scaling = 1.0 / (jnp.maximum(magnitude, 1.0) * jnp.sqrt(count * (eigen + 1e-06)))
-    phase_real = jnp.where(in_real, sums, turned) * scaling
-    phase_imag = -jnp.where(in_real, turned, sums) * scaling
-    coef = vec * phase_real - half_turned(vec, half) * (sign * phase_imag)
+    phase_r = sum_r * scaling
+    phase_i = -sum_i * scaling
+    coef = jnp.where(
+        in_real, vec_r * phase_r - vec_i * phase_i, vec_r * phase_i + vec_i * phase_r
+    )
     return coef, eigen
 
 
@@ -92,7 +103,7 @@
     return jnp.where(jnp.bitwise_and(index, lanes) == 0, value, -value)
 
 
-def write_table(table_ref, offsets_ref, freqs_ref, me, groups):
+def write_table(table_ref, offsets_ref, freqs_ref, me, groups, owners):
     rows, nfft = table_ref.shape
     half = nfft // 2
     lane = lax.broadcasted_iota(jnp.int32, (8, half), 1)
@@ -105,7 +116,7 @@
     for tile in range(rows // 8):
         tile_rows = range(8 * tile, 8 * tile + 8)
         pieces = tuple(r % (4 * groups) // (2 * groups) for r in tile_rows)
-        freq = [r // (4 * groups) * groups + r % (2 * groups) // 2 for r in tile_rows]
+        freq = [owners[r // (4 * groups)] * groups + r % (2 * groups) // 2 for r in tile_rows]
         freq_rows = jnp.full((8, half), freqs_ref[freq[0]], jnp.int32)
         for s in range(2, 8, 2):
             freq_rows = jnp.where(sub >= s, freqs_ref[freq[s]], freq_rows)
@@ -136,7 +147,7 @@
 ):
     me = lax.axis_index("blk")
     side = lax.axis_index("pts")
-    nfft, nvars, npts = snaps_ref.shape
+    nvars, nfft, npts = snaps_ref.shape
     rows = 2 * groups * nblocks
     half = rows // 2
     piece = 2 * groups
@@ -153,27 +164,36 @@
     for k in range(1, npart):
         pl.semaphore_signal(barrier, inc=1, device_id={"pts": side_peer(k)}, device_id_type=MESH)
 
-    write_table(table, offsets_ref, freqs_ref, me, groups)
-    for v in range(nvars):
-        part = jnp.dot(table[...], snaps_ref[:, v, :], precision=HIGH, preferred_element_type=jnp.float32)
-        for g in range(nblocks):
-            stage[g, :, v * npts : (v + 1) * npts] = part[2 * piece * g : 2 * piece * (g + 1)]
-
-    pl.semaphore_wait(barrier, nblocks - 1 + npart - 1)
-
-    def spectra_copy(k, slot):
-        peer = block_peer(k)
+    order = sorted(range(nblocks), key=lambda k: abs(k - nblocks // 2))
+    write_table(table, offsets_ref, freqs_ref, me, groups, [block_peer(k) for k in order])
+    snaps = jnp.concatenate([snaps_ref[v] for v in range(nvars)], axis=1)
+
+    def spectra_copy(place, slot):
         return pltpu.make_async_remote_copy(
-            src_ref=stage.at[peer], dst_ref=recv.at[slot], send_sem=send_sem.at[k],
-            recv_sem=recv_sem.at[slot], device_id={"blk": peer}, device_id_type=MESH,
+            src_ref=stage.at[place], dst_ref=recv.at[slot], send_sem=send_sem.at[place],
+            recv_sem=recv_sem.at[slot], device_id={"blk": block_peer(order[place])},
+            device_id_type=MESH,
         )
 
-    for k in range(1, nblocks):
-        spectra_copy(k, me).start()
-    recv[me] = stage[me]
+    share = nblocks // CHUNKS
+    for chunk in range(CHUNKS):
+        places = range(chunk * share, (chunk + 1) * share)
+        part = jnp.dot(
+            table[2 * piece * places[0] : 2 * piece * (places[-1] + 1), :], snaps,
+            precision=lax.Precision.HIGH, preferred_element_type=jnp.float32,
+        )
+        for at, place in enumerate(places):
+            stage[place] = part[2 * piece * at : 2 * piece * (at + 1)]
+        if chunk == 0:
+            pl.semaphore_wait(barrier, nblocks - 1 + npart - 1)
+        for place in places:
+            if order[place]:
+                spectra_copy(place, me).start()
+    recv[me] = stage[order.index(0)]
     recv[nblocks] = jnp.zeros(recv.shape[1:], jnp.float32)
-    for k in range(1, nblocks):
-        spectra_copy(k, block_peer(k)).wait_recv()
+    for place in range(nblocks):
+        if order[place]:
+            spectra_copy(place, block_peer(nblocks - order[place])).wait_recv()
 
     for ri in range(2):
         for f in range(groups):
@@ -182,13 +202,11 @@
             tail = recv[1 : nblocks + 1, piece + 2 * f + ri, :]
             spectra[at : at + nblocks, :] = own + tail
 
-    gram_all = jnp.zeros((rows, rows), jnp.float32)
-    for v in range(nvars):
-        part = spectra[:, v * npts : (v + 1) * npts]
-        gram_all = gram_all + lax.dot_general(
-            part * weights_ref[v : v + 1, :], part, (((1,), (1,)), ((), ())),
-            precision=HIGH, preferred_element_type=jnp.float32,
-        )
+    weight = jnp.concatenate([weights_ref[v : v + 1, :] for v in range(nvars)], axis=1)
+    gram_all = lax.dot_general(
+        spectra[...] * weight, spectra[...], (((1,), (1,)), ((), ())),
+        precision=HIGH, preferred_element_type=jnp.float32,
+    )
     lane = lax.broadcasted_iota(jnp.int32, (1, rows), 1)
     sign = jnp.where(lane < half, 1.0, -1.0).astype(jnp.float32)
     group_of = lax.rem(lane, half) // nblocks
@@ -234,14 +252,20 @@
     turned = -sign * half_turned(coef, half)
     pieces = [jnp.where(group_of == f, block, 0.0) for block in (coef, turned) for f in range(groups)]
     mixing = jnp.concatenate(pieces, axis=0).T
-    modes_ref[...] = jnp.dot(mixing, spectra[...], precision=HIGH, preferred_element_type=jnp.float32)
+    modes_ref[...] = jnp.dot(
+        mixing, spectra[...], precision=lax.Precision.HIGH, preferred_element_type=jnp.float32
+    )
 
     for k in range(1, nblocks):
         total_copy(k, block_peer(k)).wait_recv()
     total = jnp.sum(total_part[...], axis=0)
-    spectrum_ref[...] = energy * eigen / total
+    share_of = energy * eigen / total[:1]
+    for f in range(groups):
+        spectrum_ref[f : f + 1, :] = share_of[:, f * nblocks : (f + 1) * nblocks]
+    for place in range(nblocks):
+        if order[place]:
+            spectra_copy(place, me).wait_send()
     for k in range(1, nblocks):
-        spectra_copy(k, me).wait_send()
         total_copy(k, me).wait_send()
     for k in range(1, npart):
         gram_copy(k, side).wait_send()
@@ -263,7 +287,7 @@
         functools.partial(pipeline_kernel, nblocks, npart, groups, scale, float(nfreq * nblocks)),
         out_shape=(
             jax.ShapeDtypeStruct((rows, width), jnp.float32),
-            jax.ShapeDtypeStruct((8, rows), jnp.float32),
+            jax.ShapeDtypeStruct((groups, nblocks), jnp.float32),
         ),
         in_specs=[vmem, vmem, smem, smem],
         out_specs=(vmem, vmem),
@@ -281,9 +305,9 @@
         compiler_params=pltpu.CompilerParams(
             collective_id=0, has_side_effects=True, vmem_limit_bytes=32 * 1024 * 1024
         ),
-    )(snapshots, weights, offsets, freqs)
+    )(snapshots.transpose(1, 0, 2), weights, offsets, freqs)
     modes = modes.reshape(2, groups, nblocks, nvars, npts).transpose(1, 2, 0, 3, 4)
-    return modes, spectrum[0, :nfreq].reshape(groups, nblocks)
+    return modes, spectrum
 
 
 def solution(mesh):

time: 34.9 us -> 34.6 us (level)
  Pallas kernels: 30.8 us -> 29.7 us
  local copies, waits for them, and re-layouts: 3.24 us -> 4.04 us
    unnamed x8 -> x10, local copies, waits for them, and re-layouts: 2.5 us -> 3.99 us
    pallas_call x1, Pallas kernels: 30.8 us -> 29.7 us  [body(): pl.pallas_call(functools.partial(pipeline_kernel, nblocks, npart, groups,...]
    another operation x1 -> x0, local copies, waits for them, and re-layouts: 0.66 us -> none  [body(): return (modes, spectrum[0, :nfreq].reshape(groups, nblocks))]
where the time goes in v3:
time: 34.6 us; the launch traced here: 34.4 us
  Pallas kernels  29.7 us (86%)
  local copies, waits for them, and re-layouts  4.04 us (12%)
  between operations  0.67 us (2%)
    pallas_call x1, Pallas kernels, body(): pl.pallas_call(functools.partial(pipeline_kernel, nblocks, npart, groups,...  29.7 us
    unnamed x10, local copies, waits for them, and re-layouts  3.99 us

profile of v3, /device:TPU:0, one launch (start us, length us, event | category | flops | bytes accessed | tf_op | source)
XLA Modules:
  0.0 34.4 jit_solution(10848114641224498053)
XLA Ops:
  0.6 0.0 copy-start.3
  0.6 0.0 copy-start.2
  0.7 0.6 %copy-done.3 = s32[64]{0:T(128)S(1)} copy-done((s32[64]{0:T(128)S(1)}, s32[64]{0:T(128)}, u32[]{:S(2)}) %copy-start.3) | copy-done | bytes 280
  1.3 0.0 copy-done.2
  1.3 0.0 copy-start
  1.3 1.1 %copy-done = f32[256,5,128]{2,0,1:T(8,128)S(1)} copy-done((f32[256,5,128]{2,0,1:T(8,128)S(1)}, f32[256,5,128]{2,0,1:T(8,128)}, u32[]{:S(2)}) %copy-start) | copy-done | bytes 655384
  2.4 0.0 copy-start.1
  2.4 0.7 %copy-done.1 = f32[5,128]{1,0:T(8,128)S(1)} copy-done((f32[5,128]{1,0:T(8,128)S(1)}, f32[5,128]{1,0:T(8,128)}, u32[]{:S(2)}) %copy-start.1) | copy-done | bytes 2584
  3.1 29.7 %shard_map.59 = (f32[128,640]{1,0:T(8,128)S(1)}, f32[4,16]{1,0:T(4,128)S(1)}) custom-call(f32[5,256,128]{2,1,0:T(8,128)S(1)} %bitcast.2, f32[5,128]{1,0:T(8,128)S(1)} %copy-done.1, s32[16]{0:T(128)S(1)} %copy-done.2, s32[64]{0:T(128)S(1)} %copy-done.3), custom_call_target="tpu_custom_call" | custom-call | tf_op jit(solution)/shard_map/pallas_call | solution.py:286
  32.8 0.1 reshape.7
  32.8 1.0 %copy.7 = f32[4,16,2,5,128]{4,2,3,1,0:T(2,128)} copy(f32[4,16,2,5,128]{4,3,1,0,2:T(8,128)S(1)} %bitcast.3) | data formatting | bytes 655360
  33.8 0.6 %copy.9 = f32[4,16]{1,0:T(4,128)} copy(f32[4,16]{1,0:T(4,128)S(1)} %get-tuple-element.11) | data formatting | bytes 512
Async XLA Ops:
  0.6 0.7 %copy-start.3 = (s32[64]{0:T(128)S(1)}, s32[64]{0:T(128)}, u32[]{:S(2)}) copy-start(s32[64]{0:T(128)} %freqs_ref.1) | copy-start | bytes 772
  0.6 0.7 %copy-start.2 = (s32[16]{0:T(128)S(1)}, s32[16]{0:T(128)}, u32[]{:S(2)}) copy-start(s32[16]{0:T(128)} %offsets_ref.1) | copy-start | bytes 196
  1.3 1.1 %copy-start = (f32[256,5,128]{2,0,1:T(8,128)S(1)}, f32[256,5,128]{2,0,1:T(8,128)}, u32[]{:S(2)}) copy-start(f32[256,5,128]{2,0,1:T(8,128)} %param.4) | copy-start | bytes 1966084
  2.4 0.7 %copy-start.1 = (f32[5,128]{1,0:T(8,128)S(1)}, f32[5,128]{1,0:T(8,128)}, u32[]{:S(2)}) copy-start(f32[5,128]{1,0:T(8,128)} %weights_ref.1) | copy-start | bytes 7684

commit v4 on v3

--- a/solution.py
+++ b/solution.py
@@ -141,16 +141,35 @@
 
 def pipeline_kernel(
     nblocks, npart, groups, scale, energy,
-    snaps_ref, weights_ref, offsets_ref, freqs_ref, modes_ref, spectrum_ref,
-    table, stage, recv, spectra, gram_part, total_part,
-    send_sem, recv_sem, gram_send, gram_recv, total_send, total_recv,
+    snaps_hbm, weights_hbm, offsets_hbm, freqs_hbm, modes_ref, spectrum_ref,
+    snaps_ref, weights_ref, offsets_ref, freqs_ref,
+    table, stage, recv, halo, spectra, gram_part, total_part,
+    input_sem, send_sem, recv_sem, halo_send, halo_recv, extra_send, extra_recv,
+    gram_send, gram_recv, total_send, total_recv,
 ):
+    inputs = [
+        pltpu.make_async_copy(src, dst, input_sem.at[i])
+        for i, (src, dst) in enumerate((
+            (offsets_hbm, offsets_ref), (freqs_hbm, freqs_ref),
+            (snaps_hbm, snaps_ref), (weights_hbm, weights_ref),
+        ))
+    ]
+    for copy in inputs:
+        copy.start()
     me = lax.axis_index("blk")
     side = lax.axis_index("pts")
     nvars, nfft, npts = snaps_ref.shape
     rows = 2 * groups * nblocks
     half = rows // 2
     piece = 2 * groups
+    reach = nblocks // 2
+    upper_half = me // reach
+    within = lax.rem(me, reach)
+    far_base = (1 - upper_half) * reach
+    near_base = upper_half * reach
+    far = [far_base + lax.rem(within + j, reach) for j in range(reach)]
+    near = [near_base + lax.rem(within + j, reach) for j in range(reach)]
+    owners = far + near
 
     def block_peer(k):
         return lax.rem(me + k, nblocks)
@@ -164,42 +183,101 @@
     for k in range(1, npart):
         pl.semaphore_signal(barrier, inc=1, device_id={"pts": side_peer(k)}, device_id_type=MESH)
 
-    order = sorted(range(nblocks), key=lambda k: abs(k - nblocks // 2))
-    write_table(table, offsets_ref, freqs_ref, me, groups, [block_peer(k) for k in order])
+    inputs[0].wait()
+    inputs[1].wait()
+    write_table(table, offsets_ref, freqs_ref, me, groups, owners)
+    inputs[2].wait()
     snaps = jnp.concatenate([snaps_ref[v] for v in range(nvars)], axis=1)
 
-    def spectra_copy(place, slot):
-        return pltpu.make_async_remote_copy(
-            src_ref=stage.at[place], dst_ref=recv.at[slot], send_sem=send_sem.at[place],
-            recv_sem=recv_sem.at[slot], device_id={"blk": block_peer(order[place])},
-            device_id_type=MESH,
-        )
-
-    share = nblocks // CHUNKS
-    for chunk in range(CHUNKS):
-        places = range(chunk * share, (chunk + 1) * share)
+    def transform(first):
         part = jnp.dot(
-            table[2 * piece * places[0] : 2 * piece * (places[-1] + 1), :], snaps,
+            table[2 * piece * first : 2 * piece * (first + reach), :], snaps,
             precision=lax.Precision.HIGH, preferred_element_type=jnp.float32,
         )
-        for at, place in enumerate(places):
-            stage[place] = part[2 * piece * at : 2 * piece * (at + 1)]
-        if chunk == 0:
-            pl.semaphore_wait(barrier, nblocks - 1 + npart - 1)
-        for place in places:
-            if order[place]:
-                spectra_copy(place, me).start()
-    recv[me] = stage[order.index(0)]
-    recv[nblocks] = jnp.zeros(recv.shape[1:], jnp.float32)
-    for place in range(nblocks):
-        if order[place]:
-            spectra_copy(place, block_peer(nblocks - order[place])).wait_recv()
+        for j in range(reach):
+            at = 2 * piece * j
+            stage[first + j, 0] = part[at : at + piece]
+            stage[first + j, 1] = part[at + piece : at + 2 * piece]
+
+    def remote(src, dst, sent, received, peer):
+        return pltpu.make_async_remote_copy(
+            src_ref=src, dst_ref=dst, send_sem=sent, recv_sem=received,
+            device_id={"blk": peer}, device_id_type=MESH,
+        )
+
+    share = reach // CHUNKS
+    before = jnp.maximum(me - 1, 0)
+    after = jnp.minimum(me + 1, nblocks - 1)
+
+    def halo_copy(chunk, peer):
+        places = pl.ds(chunk * share, share)
+        return remote(
+            stage.at[places, 1], halo.at[places], halo_send.at[chunk], halo_recv.at[chunk], peer
+        )
+
+    def far_copy(j, slot, peer):
+        return remote(stage.at[j, 0], recv.at[slot, 0], send_sem.at[j], recv_sem.at[slot], peer)
+
+    def near_copy(j, slot, peer):
+        at = reach + j
+        return remote(stage.at[at], recv.at[slot], send_sem.at[at], recv_sem.at[slot], peer)
+
+    def extra_copy(j):
+        return remote(stage.at[j, 1], recv.at[reach, 1], extra_send.at[j], extra_recv.at[0], far[j])
+
+    transform(0)
+    pl.semaphore_wait(barrier, nblocks - 1 + npart - 1)
+
+    @pl.when(within != 0)
+    def _():
+        for chunk in range(CHUNKS):
+            halo_copy(chunk, before).start()
+
+    @pl.when(me == reach)
+    def _():
+        for j in range(reach):
+            extra_copy(j).start()
+
+    transform(reach)
+    for chunk in range(CHUNKS):
+        places = [(chunk * share + i, (chunk * share + i + 1) % reach) for i in range(share)]
+
+        @pl.when(within != reach - 1)
+        def _():
+            halo_copy(chunk, after).wait_recv()
+            for theirs, mine in places:
+                stage[mine, 0] = stage[mine, 0] + halo[theirs]
+
+        for _, mine in places:
+            far_copy(mine, me, far[mine]).start()
+    for j in range(1, reach):
+        near_copy(j, me, near[j]).start()
+
+    recv[me] = stage[reach]
+    empty = jnp.zeros(recv.shape[2:], jnp.float32)
+    recv[nblocks, 1] = empty
+    for i in range(1, reach):
+        recv[far_base + i, 1] = empty
+
+    @pl.when(upper_half == 1)
+    def _():
+        recv[0, 1] = empty
+
+    @pl.when(upper_half == 0)
+    def _():
+        extra_copy(0).wait_recv()
+
+    for j in range(reach):
+        far_copy(j, far[j], far[j]).wait_recv()
+    for j in range(1, reach):
+        near_copy(j, near[j], near[j]).wait_recv()
+    inputs[3].wait()
 
     for ri in range(2):
         for f in range(groups):
             at = (ri * groups + f) * nblocks
-            own = recv[0:nblocks, 2 * f + ri, :]
-            tail = recv[1 : nblocks + 1, piece + 2 * f + ri, :]
+            own = recv[0:nblocks, 0, 2 * f + ri, :]
+            tail = recv[1 : nblocks + 1, 1, 2 * f + ri, :]
             spectra[at : at + nblocks, :] = own + tail
 
     weight = jnp.concatenate([weights_ref[v : v + 1, :] for v in range(nvars)], axis=1)
@@ -262,9 +340,21 @@
     share_of = energy * eigen / total[:1]
     for f in range(groups):
         spectrum_ref[f : f + 1, :] = share_of[:, f * nblocks : (f + 1) * nblocks]
-    for place in range(nblocks):
-        if order[place]:
-            spectra_copy(place, me).wait_send()
+    for j in range(reach):
+        far_copy(j, me, far[j]).wait_send()
+    for j in range(1, reach):
+        near_copy(j, me, near[j]).wait_send()
+
+    @pl.when(within != 0)
+    def _():
+        for chunk in range(CHUNKS):
+            halo_copy(chunk, before).wait_send()
+
+    @pl.when(me == reach)
+    def _():
+        for j in range(reach):
+            extra_copy(j).wait_send()
+
     for k in range(1, nblocks):
         total_copy(k, me).wait_send()
     for k in range(1, npart):
@@ -282,23 +372,31 @@
     scale = 1.0 / (nblocks * nvars * npts * npart)
     dma = pltpu.SemaphoreType.DMA
     vmem = pl.BlockSpec(memory_space=pltpu.VMEM)
-    smem = pl.BlockSpec(memory_space=pltpu.SMEM)
+    far_memory = pl.BlockSpec(memory_space=pltpu.HBM)
     modes, spectrum = pl.pallas_call(
         functools.partial(pipeline_kernel, nblocks, npart, groups, scale, float(nfreq * nblocks)),
         out_shape=(
             jax.ShapeDtypeStruct((rows, width), jnp.float32),
             jax.ShapeDtypeStruct((groups, nblocks), jnp.float32),
         ),
-        in_specs=[vmem, vmem, smem, smem],
+        in_specs=[far_memory] * 4,
         out_specs=(vmem, vmem),
         scratch_shapes=[
+            pltpu.VMEM((nvars, nfft, npts), jnp.float32),
+            pltpu.VMEM((nvars, npts), jnp.float32),
+            pltpu.SMEM((nblocks,), jnp.int32),
+            pltpu.SMEM((nfreq,), jnp.int32),
             pltpu.VMEM((2 * rows, nfft), jnp.float32),
-            pltpu.VMEM((nblocks, 4 * groups, width), jnp.float32),
-            pltpu.VMEM((nblocks + 1, 4 * groups, width), jnp.float32),
+            pltpu.VMEM((nblocks, 2, 2 * groups, width), jnp.float32),
+            pltpu.VMEM((nblocks + 1, 2, 2 * groups, width), jnp.float32),
+            pltpu.VMEM((nblocks // 2, 2 * groups, width), jnp.float32),
             pltpu.VMEM((rows, width), jnp.float32),
             pltpu.VMEM((npart, nblocks, rows), jnp.float32),
             pltpu.VMEM((nblocks, 8, rows), jnp.float32),
+            dma((4,)),
             dma((nblocks,)), dma((nblocks,)),
+            dma((CHUNKS,)), dma((CHUNKS,)),
+            dma((nblocks // 2,)), dma((1,)),
             dma((npart,)), dma((npart,)),
             dma((nblocks,)), dma((nblocks,)),
         ],

time: 34.6 us -> 33.4 us (0.965)
  Pallas kernels: 29.7 us -> 28.5 us
    pallas_call x1, Pallas kernels: 29.7 us -> 28.5 us  [body(): pl.pallas_call(functools.partial(pipeline_kernel, nblocks, npart, groups,...]
where the time goes in v4:
time: 33.4 us; the launch traced here: 33.2 us
  Pallas kernels  28.5 us (85%)
  local copies, waits for them, and re-layouts  4.04 us (12%)
  between operations  0.67 us (2%)
    pallas_call x1, Pallas kernels, body(): pl.pallas_call(functools.partial(pipeline_kernel, nblocks, npart, groups,...  28.5 us
    unnamed x10, local copies, waits for them, and re-layouts  3.99 us

profile of v4, /device:TPU:0, one launch (start us, length us, event | category | flops | bytes accessed | tf_op | source)
XLA Modules:
  0.0 33.2 jit_solution(14973789162291517832)
XLA Ops:
  0.6 0.0 copy-start.3
  0.6 0.0 copy-start.2
  0.7 0.6 %copy-done.3 = s32[64]{0:T(128)S(1)} copy-done((s32[64]{0:T(128)S(1)}, s32[64]{0:T(128)}, u32[]{:S(2)}) %copy-start.3) | copy-done | bytes 280
  1.3 0.0 copy-done.2
  1.3 0.0 copy-start
  1.3 1.1 %copy-done = f32[256,5,128]{2,0,1:T(8,128)S(1)} copy-done((f32[256,5,128]{2,0,1:T(8,128)S(1)}, f32[256,5,128]{2,0,1:T(8,128)}, u32[]{:S(2)}) %copy-start) | copy-done | bytes 655384
  2.4 0.0 copy-start.1
  2.4 0.7 %copy-done.1 = f32[5,128]{1,0:T(8,128)S(1)} copy-done((f32[5,128]{1,0:T(8,128)S(1)}, f32[5,128]{1,0:T(8,128)}, u32[]{:S(2)}) %copy-start.1) | copy-done | bytes 2584
  3.1 28.5 %shard_map.59 = (f32[128,640]{1,0:T(8,128)S(1)}, f32[4,16]{1,0:T(4,128)S(1)}) custom-call(f32[5,256,128]{2,1,0:T(8,128)S(1)} %bitcast.2, f32[5,128]{1,0:T(8,128)S(1)} %copy-done.1, s32[16]{0:T(128)S(1)} %copy-done.2, s32[64]{0:T(128)S(1)} %copy-done.3), custom_call_target="tpu_custom_call" | custom-call | tf_op jit(solution)/shard_map/pallas_call | solution.py:376
  31.6 0.1 reshape.7
  31.7 1.0 %copy.7 = f32[4,16,2,5,128]{4,2,3,1,0:T(2,128)} copy(f32[4,16,2,5,128]{4,3,1,0,2:T(8,128)S(1)} %bitcast.3) | data formatting | bytes 655360
  32.6 0.6 %copy.9 = f32[4,16]{1,0:T(4,128)} copy(f32[4,16]{1,0:T(4,128)S(1)} %get-tuple-element.11) | data formatting | bytes 512
Async XLA Ops:
  0.6 0.7 %copy-start.3 = (s32[64]{0:T(128)S(1)}, s32[64]{0:T(128)}, u32[]{:S(2)}) copy-start(s32[64]{0:T(128)} %freqs_hbm.1) | copy-start | bytes 772
  0.6 0.7 %copy-start.2 = (s32[16]{0:T(128)S(1)}, s32[16]{0:T(128)}, u32[]{:S(2)}) copy-start(s32[16]{0:T(128)} %offsets_hbm.1) | copy-start | bytes 196
  1.3 1.1 %copy-start = (f32[256,5,128]{2,0,1:T(8,128)S(1)}, f32[256,5,128]{2,0,1:T(8,128)}, u32[]{:S(2)}) copy-start(f32[256,5,128]{2,0,1:T(8,128)} %param.4) | copy-start | bytes 1966084
  2.4 0.7 %copy-start.1 = (f32[5,128]{1,0:T(8,128)S(1)}, f32[5,128]{1,0:T(8,128)}, u32[]{:S(2)}) copy-start(f32[5,128]{1,0:T(8,128)} %weights_hbm.1) | copy-start | bytes 7684

commit v5 on v4

--- a/solution.py
+++ b/solution.py
@@ -143,7 +143,7 @@
     nblocks, npart, groups, scale, energy,
     snaps_hbm, weights_hbm, offsets_hbm, freqs_hbm, modes_ref, spectrum_ref,
     snaps_ref, weights_ref, offsets_ref, freqs_ref,
-    table, stage, recv, halo, spectra, gram_part, total_part,
+    table, stage, recv, halo, spectra, order, gram_part, total_part,
     input_sem, send_sem, recv_sem, halo_send, halo_recv, extra_send, extra_recv,
     gram_send, gram_recv, total_send, total_recv,
 ):
@@ -239,6 +239,8 @@
             extra_copy(j).start()
 
     transform(reach)
+    for j in range(1, share + 1):
+        near_copy(j, me, near[j]).start()
     for chunk in range(CHUNKS):
         places = [(chunk * share + i, (chunk * share + i + 1) % reach) for i in range(share)]
 
@@ -250,7 +252,7 @@
 
         for _, mine in places:
             far_copy(mine, me, far[mine]).start()
-    for j in range(1, reach):
+    for j in range(share + 1, reach):
         near_copy(j, me, near[j]).start()
 
     recv[me] = stage[reach]
@@ -273,12 +275,8 @@
         near_copy(j, near[j], near[j]).wait_recv()
     inputs[3].wait()
 
-    for ri in range(2):
-        for f in range(groups):
-            at = (ri * groups + f) * nblocks
-            own = recv[0:nblocks, 0, 2 * f + ri, :]
-            tail = recv[1 : nblocks + 1, 1, 2 * f + ri, :]
-            spectra[at : at + nblocks, :] = own + tail
+    combined = recv[0:nblocks, 0] + recv[1 : nblocks + 1, 1]
+    spectra[...] = combined.reshape(rows, nvars * npts)
 
     weight = jnp.concatenate([weights_ref[v : v + 1, :] for v in range(nvars)], axis=1)
     gram_all = lax.dot_general(
@@ -288,10 +286,12 @@
     lane = lax.broadcasted_iota(jnp.int32, (1, rows), 1)
     sign = jnp.where(lane < half, 1.0, -1.0).astype(jnp.float32)
     group_of = lax.rem(lane, half) // nblocks
+    arrival = lax.rem(lane, nblocks) * piece + 2 * group_of + jnp.where(lane < half, 0, 1)
+    order[...] = lane_gather(gram_all, arrival).reshape(order.shape)
     gram = jnp.zeros((nblocks, rows), jnp.float32)
     for f in range(groups):
-        upper = gram_all[f * nblocks : (f + 1) * nblocks]
-        lower = gram_all[half + f * nblocks : half + (f + 1) * nblocks]
+        upper = order[:, 2 * f, :]
+        lower = order[:, 2 * f + 1, :]
         gram = jnp.where(group_of == f, upper + sign * pltpu.roll(lower, half, 1), gram)
     gram_part[side] = gram * scale
 
@@ -328,8 +328,10 @@
     coef, eigen = jacobi_on_lanes(gram, nblocks, groups)
 
     turned = -sign * half_turned(coef, half)
-    pieces = [jnp.where(group_of == f, block, 0.0) for block in (coef, turned) for f in range(groups)]
-    mixing = jnp.concatenate(pieces, axis=0).T
+    for ri, block in enumerate((coef, turned)):
+        for f in range(groups):
+            order[:, 2 * f + ri, :] = jnp.where(group_of == f, block, 0.0)
+    mixing = order[...].reshape(rows, rows).T
     modes_ref[...] = jnp.dot(
         mixing, spectra[...], precision=lax.Precision.HIGH, preferred_element_type=jnp.float32
     )
@@ -391,6 +393,7 @@
             pltpu.VMEM((nblocks + 1, 2, 2 * groups, width), jnp.float32),
             pltpu.VMEM((nblocks // 2, 2 * groups, width), jnp.float32),
             pltpu.VMEM((rows, width), jnp.float32),
+            pltpu.VMEM((nblocks, 2 * groups, rows), jnp.float32),
             pltpu.VMEM((npart, nblocks, rows), jnp.float32),
             pltpu.VMEM((nblocks, 8, rows), jnp.float32),
             dma((4,)),
@@ -401,7 +404,7 @@
             dma((nblocks,)), dma((nblocks,)),
         ],
         compiler_params=pltpu.CompilerParams(
-            collective_id=0, has_side_effects=True, vmem_limit_bytes=32 * 1024 * 1024
+            collective_id=0, has_side_effects=True, vmem_limit_bytes=60 * 1024 * 1024
         ),
     )(snapshots.transpose(1, 0, 2), weights, offsets, freqs)
     modes = modes.reshape(2, groups, nblocks, nvars, npts).transpose(1, 2, 0, 3, 4)

time: 33.4 us -> 30.7 us (0.919)
  local copies, waits for them, and re-layouts: 4.04 us -> 2.58 us
  Pallas kernels: 28.5 us -> 27.3 us
    unnamed x10 -> x4, local copies, waits for them, and re-layouts: 3.99 us -> 1.56 us
    pallas_call x1, Pallas kernels: 28.5 us -> 27.3 us  [body(): pl.pallas_call(functools.partial(pipeline_kernel, nblocks, npart, groups,...]
    reshape x1, local copies, waits for them, and re-layouts: 0.05 us -> 1.02 us  [body(): modes.reshape(2, groups, nblocks, nvars, npts).transpose(1, 2, 0, 3, 4)]
where the time goes in v5:
time: 30.7 us; the launch traced here: 30.5 us
  Pallas kernels  27.3 us (89%)
  local copies, waits for them, and re-layouts  2.58 us (8%)
  between operations  0.65 us (2%)
    pallas_call x1, Pallas kernels, body(): pl.pallas_call(functools.partial(pipeline_kernel, nblocks, npart, groups,...  27.3 us
    unnamed x4, local copies, waits for them, and re-layouts  1.56 us
    reshape x1, local copies, waits for them, and re-layouts, body(): modes.reshape(2, groups, nblocks, nvars, npts).transpose(1, 2, 0, 3, 4)  1.02 us

profile of v5, /device:TPU:0, one launch (start us, length us, event | category | flops | bytes accessed | tf_op | source)
XLA Modules:
  0.0 30.5 jit_solution(18225645309738754479)
XLA Ops:
  0.6 27.3 %shard_map.59 = (f32[128,640]{1,0:T(8,128)}, f32[4,16]{1,0:T(4,128)}) custom-call(f32[5,256,128]{2,1,0:T(8,128)} %bitcast.3, f32[5,128]{1,0:T(8,128)} %weights_hbm.1, s32[16]{0:T(128)} %offsets_hbm.1, s32[64]{0:T(128)} %freqs_hbm.1), custom_call_target="tpu_custom_call" | custom-call | tf_op jit(solution)/shard_map/pallas_call | solution.py:378
  27.9 1.0 %reshape.7 = f32[2,4,16,5,128]{4,3,2,1,0:T(8,128)S(1)} reshape(f32[128,640]{1,0:T(8,128)} %get-tuple-element.4) | data formatting | bytes 655360 | tf_op jit(solution)/shard_map/reshape | solution.py:410
  28.9 0.0 copy-start
  28.9 1.0 %copy.7 = f32[4,16,2,5,128]{4,2,3,1,0:T(2,128)} copy(f32[4,16,2,5,128]{4,3,1,0,2:T(8,128)S(1)} %bitcast.2) | data formatting | bytes 655360
  29.9 0.0 copy-done
  29.9 0.6 %copy.9 = f32[4,16]{1,0:T(4,128)} copy(f32[4,16]{1,0:T(4,128)S(1)} %copy-done) | data formatting | bytes 512
Async XLA Ops:
  28.9 1.0 %copy-start = (f32[4,16]{1,0:T(4,128)S(1)}, f32[4,16]{1,0:T(4,128)}, u32[]{:S(2)}) copy-start(f32[4,16]{1,0:T(4,128)} %get-tuple-element.11) | copy-start | bytes 772

commit v6 on v5

--- a/solution.py
+++ b/solution.py
@@ -332,9 +332,14 @@
         for f in range(groups):
             order[:, 2 * f + ri, :] = jnp.where(group_of == f, block, 0.0)
     mixing = order[...].reshape(rows, rows).T
-    modes_ref[...] = jnp.dot(
+    modes = jnp.dot(
         mixing, spectra[...], precision=lax.Precision.HIGH, preferred_element_type=jnp.float32
     )
+    for v in range(nvars):
+        for ri in range(2):
+            modes_ref[pl.ds(2 * v + ri, half, stride=2 * nvars), :] = modes[
+                ri * half : (ri + 1) * half, v * npts : (v + 1) * npts
+            ]
 
     for k in range(1, nblocks):
         total_copy(k, block_peer(k)).wait_recv()
@@ -378,7 +383,7 @@
     modes, spectrum = pl.pallas_call(
         functools.partial(pipeline_kernel, nblocks, npart, groups, scale, float(nfreq * nblocks)),
         out_shape=(
-            jax.ShapeDtypeStruct((rows, width), jnp.float32),
+            jax.ShapeDtypeStruct((rows * nvars, npts), jnp.float32),
             jax.ShapeDtypeStruct((groups, nblocks), jnp.float32),
         ),
         in_specs=[far_memory] * 4,
@@ -407,7 +412,7 @@
             collective_id=0, has_side_effects=True, vmem_limit_bytes=60 * 1024 * 1024
         ),
     )(snapshots.transpose(1, 0, 2), weights, offsets, freqs)
-    modes = modes.reshape(2, groups, nblocks, nvars, npts).transpose(1, 2, 0, 3, 4)
+    modes = modes.reshape(groups, nblocks, nvars, 2, npts).transpose(0, 1, 3, 2, 4)
     return modes, spectrum
 
 

time: 30.7 us -> 30.4 us (level)
    reshape x1 -> x0, local copies, waits for them, and re-layouts: 1.02 us -> none  [body(): modes.reshape(2, groups, nblocks, nvars, npts).transpose(1, 2, 0, 3, 4)]
    unnamed x4, local copies, waits for them, and re-layouts: 1.56 us -> 2.32 us
where the time goes in v6:
time: 30.4 us; the launch traced here: 30.2 us
  Pallas kernels  27.3 us (90%)
  local copies, waits for them, and re-layouts  2.32 us (8%)
  between operations  0.65 us (2%)
    pallas_call x1, Pallas kernels, body(): pl.pallas_call(functools.partial(pipeline_kernel, nblocks, npart, groups,...  27.3 us
    unnamed x4, local copies, waits for them, and re-layouts  2.32 us

profile of v6, /device:TPU:0, one launch (start us, length us, event | category | flops | bytes accessed | tf_op | source)
XLA Modules:
  0.0 30.2 jit_solution(6773417627652560130)
XLA Ops:
  0.6 27.3 %shard_map.59 = (f32[640,128]{1,0:T(8,128)}, f32[4,16]{1,0:T(4,128)}) custom-call(f32[5,256,128]{2,1,0:T(8,128)} %bitcast.4, f32[5,128]{1,0:T(8,128)} %weights_hbm.1, s32[16]{0:T(128)} %offsets_hbm.1, s32[64]{0:T(128)} %freqs_hbm.1), custom_call_target="tpu_custom_call" | custom-call | tf_op jit(solution)/shard_map/pallas_call | solution.py:383
  27.9 0.0 copy-start
  27.9 1.7 %copy.8 = f32[4,16,2,5,128]{4,2,3,1,0:T(2,128)} copy(f32[4,16,2,5,128]{4,2,3,1,0:T(2,128)} %bitcast.5) | data formatting | bytes 655360
  29.7 0.0 copy-done
  29.7 0.6 %copy.9 = f32[4,16]{1,0:T(4,128)} copy(f32[4,16]{1,0:T(4,128)S(1)} %copy-done) | data formatting | bytes 512
Async XLA Ops:
  27.9 1.8 %copy-start = (f32[4,16]{1,0:T(4,128)S(1)}, f32[4,16]{1,0:T(4,128)}, u32[]{:S(2)}) copy-start(f32[4,16]{1,0:T(4,128)} %get-tuple-element.9) | copy-start | bytes 772

commit v7 on v5

--- a/solution.py
+++ b/solution.py
@@ -141,10 +141,10 @@
 
 def pipeline_kernel(
     nblocks, npart, groups, scale, energy,
-    snaps_hbm, weights_hbm, offsets_hbm, freqs_hbm, modes_ref, spectrum_ref,
+    snaps_hbm, weights_hbm, offsets_hbm, freqs_hbm, spectra_hbm, mixing_ref, spectrum_ref,
     snaps_ref, weights_ref, offsets_ref, freqs_ref,
     table, stage, recv, halo, spectra, order, gram_part, total_part,
-    input_sem, send_sem, recv_sem, halo_send, halo_recv, extra_send, extra_recv,
+    input_sem, output_sem, send_sem, recv_sem, halo_send, halo_recv, extra_send, extra_recv,
     gram_send, gram_recv, total_send, total_recv,
 ):
     inputs = [
@@ -277,6 +277,8 @@
 
     combined = recv[0:nblocks, 0] + recv[1 : nblocks + 1, 1]
     spectra[...] = combined.reshape(rows, nvars * npts)
+    spectra_out = pltpu.make_async_copy(spectra, spectra_hbm, output_sem.at[0])
+    spectra_out.start()
 
     weight = jnp.concatenate([weights_ref[v : v + 1, :] for v in range(nvars)], axis=1)
     gram_all = lax.dot_general(
@@ -331,10 +333,7 @@
     for ri, block in enumerate((coef, turned)):
         for f in range(groups):
             order[:, 2 * f + ri, :] = jnp.where(group_of == f, block, 0.0)
-    mixing = order[...].reshape(rows, rows).T
-    modes_ref[...] = jnp.dot(
-        mixing, spectra[...], precision=lax.Precision.HIGH, preferred_element_type=jnp.float32
-    )
+    mixing_ref[...] = order[...].reshape(rows, rows).T
 
     for k in range(1, nblocks):
         total_copy(k, block_peer(k)).wait_recv()
@@ -342,6 +341,7 @@
     share_of = energy * eigen / total[:1]
     for f in range(groups):
         spectrum_ref[f : f + 1, :] = share_of[:, f * nblocks : (f + 1) * nblocks]
+    spectra_out.wait()
     for j in range(reach):
         far_copy(j, me, far[j]).wait_send()
     for j in range(1, reach):
@@ -361,6 +361,22 @@
         total_copy(k, me).wait_send()
     for k in range(1, npart):
         gram_copy(k, side).wait_send()
+
+
+def modes_kernel(nvars, spectra_ref, mixing_ref, share_ref, modes_ref, spectrum_ref):
+    rows, width = spectra_ref.shape
+    half = rows // 2
+    npts = width // nvars
+    spectrum_ref[...] = share_ref[...]
+    modes = jnp.dot(
+        mixing_ref[...], spectra_ref[...], precision=lax.Precision.HIGH,
+        preferred_element_type=jnp.float32,
+    )
+    for v in range(nvars):
+        for ri in range(2):
+            modes_ref[pl.ds(2 * v + ri, half, stride=2 * nvars), :] = modes[
+                ri * half : (ri + 1) * half, v * npts : (v + 1) * npts
+            ]
 
 
 def body(snapshots, weights, offsets, freqs):
@@ -375,14 +391,15 @@
     dma = pltpu.SemaphoreType.DMA
     vmem = pl.BlockSpec(memory_space=pltpu.VMEM)
     far_memory = pl.BlockSpec(memory_space=pltpu.HBM)
-    modes, spectrum = pl.pallas_call(
+    spectra, mixing, share = pl.pallas_call(
         functools.partial(pipeline_kernel, nblocks, npart, groups, scale, float(nfreq * nblocks)),
         out_shape=(
             jax.ShapeDtypeStruct((rows, width), jnp.float32),
+            jax.ShapeDtypeStruct((rows, rows), jnp.float32),
             jax.ShapeDtypeStruct((groups, nblocks), jnp.float32),
         ),
         in_specs=[far_memory] * 4,
-        out_specs=(vmem, vmem),
+        out_specs=(far_memory, vmem, vmem),
         scratch_shapes=[
             pltpu.VMEM((nvars, nfft, npts), jnp.float32),
             pltpu.VMEM((nvars, npts), jnp.float32),
@@ -396,7 +413,7 @@
             pltpu.VMEM((nblocks, 2 * groups, rows), jnp.float32),
             pltpu.VMEM((npart, nblocks, rows), jnp.float32),
             pltpu.VMEM((nblocks, 8, rows), jnp.float32),
-            dma((4,)),
+            dma((4,)), dma((1,)),
             dma((nblocks,)), dma((nblocks,)),
             dma((CHUNKS,)), dma((CHUNKS,)),
             dma((nblocks // 2,)), dma((1,)),
@@ -407,7 +424,17 @@
             collective_id=0, has_side_effects=True, vmem_limit_bytes=60 * 1024 * 1024
         ),
     )(snapshots.transpose(1, 0, 2), weights, offsets, freqs)
-    modes = modes.reshape(2, groups, nblocks, nvars, npts).transpose(1, 2, 0, 3, 4)
+    modes, spectrum = pl.pallas_call(
+        functools.partial(modes_kernel, nvars),
+        out_shape=(
+            jax.ShapeDtypeStruct((rows * nvars, npts), jnp.float32),
+            jax.ShapeDtypeStruct((groups, nblocks), jnp.float32),
+        ),
+        in_specs=[vmem] * 3,
+        out_specs=(vmem, vmem),
+        compiler_params=pltpu.CompilerParams(vmem_limit_bytes=60 * 1024 * 1024),
+    )(spectra, mixing, share)
+    modes = modes.reshape(groups, nblocks, nvars, 2, npts).transpose(0, 1, 3, 2, 4)
     return modes, spectrum
 
 

time: 30.7 us -> 30 us (0.977)
  local copies, waits for them, and re-layouts: 2.58 us -> 0 us
  Pallas kernels: 27.3 us -> 29.2 us
    pallas_call x0 -> x1, Pallas kernels: none -> 2.04 us  [body(): pl.pallas_call(functools.partial(modes_kernel, nvars), out_shape=(jax.Sha...]
    unnamed x4 -> x0, local copies, waits for them, and re-layouts: 1.56 us -> none
    reshape x1 -> x0, local copies, waits for them, and re-layouts: 1.02 us -> none  [body(): modes.reshape(2, groups, nblocks, nvars, npts).transpose(1, 2, 0, 3, 4)]
where the time goes in v7:
time: 30 us; the launch traced here: 29.9 us
  Pallas kernels  29.2 us (97%)
  between operations  0.64 us (2%)
    pallas_call x1, Pallas kernels, body(): pl.pallas_call(functools.partial(pipeline_kernel, nblocks, npart, groups,...  27.2 us
    pallas_call x1, Pallas kernels, body(): pl.pallas_call(functools.partial(modes_kernel, nvars), out_shape=(jax.Sha...  2.04 us

profile of v7, /device:TPU:0, one launch (start us, length us, event | category | flops | bytes accessed | tf_op | source)
XLA Modules:
  0.0 29.9 jit_solution(18404140926010810217)
XLA Ops:
  0.6 27.2 %shard_map.59 = (f32[128,640]{1,0:T(8,128)}, f32[128,128]{1,0:T(8,128)}, f32[4,16]{1,0:T(4,128)}) custom-call(f32[5,256,128]{2,1,0:T(8,128)} %bitcast.4, f32[5,128]{1,0:T(8,128)} %weights_hbm.1, s32[16]{0:T(128)} %offsets_hbm.1, s32[64]{0:T(128)} %freqs_hbm.1), custom_call_target="tpu_custom_call" | custom-call | tf_op jit(solution)/shard_map/pallas_call | solution.py:394
  27.8 2.0 %shard_map.60 = (f32[640,128]{1,0:T(8,128)}, f32[4,16]{1,0:T(4,128)}) custom-call(f32[128,640]{1,0:T(8,128)} %get-tuple-element.7.spectra_ref, f32[128,128]{1,0:T(8,128)} %get-tuple-element.8.mixing_ref, f32[4,16]{1,0:T(4,128)} %get-tuple-element.9.share_ref), custom_call_target="tpu_custom_call" | custom-call | tf_op jit(solution)/shard_map/pallas_call | solution.py:427

commit v8 on v7

--- a/solution.py
+++ b/solution.py
@@ -13,7 +13,7 @@
 
 HIGH = lax.Precision.HIGHEST
 DAMPING = 0.01
-CHUNKS = 2
+CHUNKS = 4
 MESH = pl.DeviceIdType.MESH
 
 
@@ -83,7 +83,7 @@
         return vec_r, vec_i, prod_r, prod_i, diag, following
 
     state = (eye, jnp.zeros_like(eye), prod_r, prod_i, diag, partner_of(0))
-    state = lax.fori_loop(0, SWEEPS * (count - 1), advance, state, unroll=3)
+    state = lax.fori_loop(0, SWEEPS * (count - 1), advance, state, unroll=6)
     vec_r, vec_i, _, _, eigen, _ = state
     sum_r = jnp.sum(vec_r, axis=0, keepdims=True)
     sum_i = jnp.sum(vec_i, axis=0, keepdims=True)

time: 30 us -> 30.1 us (level)
  no operation moved by 1% of the time
where the time goes in v8:
time: 30.1 us; the launch traced here: 29.9 us
  Pallas kernels  29.3 us (97%)
  between operations  0.64 us (2%)
    pallas_call x1, Pallas kernels, body(): pl.pallas_call(functools.partial(pipeline_kernel, nblocks, npart, groups,...  27.2 us
    pallas_call x1, Pallas kernels, body(): pl.pallas_call(functools.partial(modes_kernel, nvars), out_shape=(jax.Sha...  2.04 us

profile of v8, /device:TPU:0, one launch (start us, length us, event | category | flops | bytes accessed | tf_op | source)
XLA Modules:
  0.0 29.9 jit_solution(10496425244656872373)
XLA Ops:
  0.6 27.2 %shard_map.59 = (f32[128,640]{1,0:T(8,128)}, f32[128,128]{1,0:T(8,128)}, f32[4,16]{1,0:T(4,128)}) custom-call(f32[5,256,128]{2,1,0:T(8,128)} %bitcast.4, f32[5,128]{1,0:T(8,128)} %weights_hbm.1, s32[16]{0:T(128)} %offsets_hbm.1, s32[64]{0:T(128)} %freqs_hbm.1), custom_call_target="tpu_custom_call" | custom-call | tf_op jit(solution)/shard_map/pallas_call | solution.py:394
  27.9 2.0 %shard_map.60 = (f32[640,128]{1,0:T(8,128)}, f32[4,16]{1,0:T(4,128)}) custom-call(f32[128,640]{1,0:T(8,128)} %get-tuple-element.7.spectra_ref, f32[128,128]{1,0:T(8,128)} %get-tuple-element.8.mixing_ref, f32[4,16]{1,0:T(4,128)} %get-tuple-element.9.share_ref), custom_call_target="tpu_custom_call" | custom-call | tf_op jit(solution)/shard_map/pallas_call | solution.py:427
